TPU v7x, 512 devices: a whole 4x8x8 slice. The times are simulated.
512 devices in a mesh: ctx: 64 (over y_hi, z, x), head: 8 (over y_lo, core).
Axes of the slice: x: 4, y: 8 (y_hi: 2, y_lo: 4; y = y_hi * 4 + y_lo), z: 8, core: 2. Of those that a mesh axis runs over, the one named last changes fastest.
Arguments:
- query: bfloat16 [16384, 8192], P(('ctx', 'head')), may hold values from -136 to 136
- d_out: bfloat16 [16384, 8192], P(('ctx', 'head')), may hold values from -6 to 6
- keys_img: bfloat16 [65536, 1024], P('ctx', 'head'), may hold values from -6 to 6
- values_img: bfloat16 [65536, 1024], P('ctx', 'head'), may hold values from -6 to 6
- image_of: int32 [16384], P('ctx'), may hold values from 0 to 63, as said below
- owner: int32 [64], replicated, may hold values from 0 to 63, as said below
Outputs:
- attended: bfloat16 [16384, 8192], P(('ctx', 'head'))
- d_query: bfloat16 [16384, 8192], P(('ctx', 'head'))
- d_keys: float32 [65536, 1024], P('ctx', 'head')
- d_values: float32 [65536, 1024], P('ctx', 'head')
Inputs may be any that keep to these rules, and one draw needn't show every extreme that they name: image_of never falls along the tokens; image j's first token is j * 256 plus an offset below 256 (image 0 at 0), so the c-th block of 256 tokens reads only images c - 1 and c. owner is a permutation that keeps or exchanges each pair of images 2k, 2k + 1.
All inputs are finite; a program needn't handle non-finite values.
Results may differ from a plain program's by a relative error of at most 0.03.
Values may be sent and summed in bfloat16 or wider, within the bound.
A program may use at most 64 MiB of HBM per device.

v0:
```python
import jax
import jax.numpy as jnp
from jax import lax
from jax.sharding import PartitionSpec as P

H = 64
KVH = 8
HD = 128


NEG_FILL = -1e30


def partner_2(value, axis, apart):
    return lax.ppermute(value, axis, [(i, i ^ 1 << apart) for i in range(lax.axis_size(axis))])


def passed_along(value, axis, by):
    size = lax.axis_size(axis)
    pairs = [(i, i + by) for i in range(size) if 0 <= i + by < size]
    return lax.ppermute(value, axis, pairs)


def pair_weights(queries, key_cols, allowed, factor):
    scores = (
        jnp.einsum("tad,kd->atk", queries, key_cols, preferred_element_type=jnp.float32) * factor
    )
    scores = jnp.where(allowed[None], scores, NEG_FILL)
    top = jnp.max(scores, axis=-1, keepdims=True)
    expo = jnp.exp(scores - top)
    weights = expo / jnp.sum(expo, axis=-1, keepdims=True)
    return (weights, weights.astype(jnp.bfloat16))


def pair_output(probs, value_cols):
    return jnp.einsum("atk,kd->tad", probs, value_cols, preferred_element_type=jnp.float32).astype(
        jnp.bfloat16
    )


def pair_grads(queries, grads, outputs, weights, probs, key_cols, value_cols, factor):
    delta_sum = jnp.sum(grads.astype(jnp.float32) * outputs.astype(jnp.float32), axis=-1)
    dprob = jnp.einsum("tad,kd->atk", grads, value_cols, preferred_element_type=jnp.float32)
    dscore = (weights * (dprob - jnp.transpose(delta_sum)[:, :, None])).astype(jnp.bfloat16)
    dquery = (
        jnp.einsum("atk,kd->tad", dscore, key_cols, preferred_element_type=jnp.float32) * factor
    ).astype(jnp.bfloat16)
    dkey = jnp.einsum("atk,tad->kd", dscore, queries, preferred_element_type=jnp.float32) * factor
    dvalue = jnp.einsum("atk,tad->kd", probs, grads, preferred_element_type=jnp.float32)
    return (dquery, dkey, dvalue)


def per_device(query, d_out, keys_img, values_img, image_of, owner):
    head_count = lax.axis_size("head")
    local_heads = H // head_count
    group_size = H // KVH
    factor = HD ** (-0.5)
    place = lax.axis_index("ctx")
    q_local, g_local = (
        lax.all_to_all(query, "head", split_axis=1, concat_axis=0, tiled=True),
        lax.all_to_all(d_out, "head", split_axis=1, concat_axis=0, tiled=True),
    )
    tok_rows = q_local.shape[0]
    span = keys_img.shape[0]
    width = keys_img.shape[1]
    flipped = owner[place] != place
    partner = partner_2((keys_img, values_img), "ctx", 0)
    send_key = jnp.where(flipped, partner[0], keys_img)
    send_value = jnp.where(flipped, partner[1], values_img)
    lower_one = passed_along((send_key, send_value), "ctx", 1)
    key_pair = jnp.concatenate([lower_one[0], send_key], axis=0)
    value_pair = jnp.concatenate([lower_one[1], send_value], axis=0)
    allowed = jnp.concatenate(
        [
            jnp.broadcast_to((image_of == place - 1)[:, None], (tok_rows, span)),
            jnp.broadcast_to((image_of == place)[:, None], (tok_rows, span)),
        ],
        axis=1,
    )
    pair_count = local_heads // 2

    def pieces(pair_index):
        column = pair_index * 2 * HD
        queries = lax.dynamic_slice_in_dim(q_local, column, 2 * HD, 1).reshape(tok_rows, 2, HD)
        grads = lax.dynamic_slice_in_dim(g_local, column, 2 * HD, 1).reshape(tok_rows, 2, HD)
        kv_column = pair_index * 2 // group_size * HD
        return (queries, grads, kv_column, key_pair, value_pair)

    def add_columns(total, term):
        return total + term

    def merge_parts(parts):
        return jnp.moveaxis(parts, 0, 1).reshape(tok_rows, local_heads * HD)

    empty = jnp.zeros((2 * span, width), jnp.float32)
    pair_ids = jnp.arange(pair_count)

    def joint_step(carry, pair_index):
        queries, grads, kv_column, key_cols, value_cols = pieces(pair_index)
        weights, probs = pair_weights(queries, key_cols, allowed, factor)
        outputs = pair_output(probs, value_cols)
        dquery, dkey, dvalue = pair_grads(
            queries, grads, outputs, weights, probs, key_cols, value_cols, factor
        )
        key_total = add_columns(carry[0], dkey)
        value_total = add_columns(carry[1], dvalue)
        return (
            (key_total, value_total),
            (outputs.reshape(tok_rows, 2 * HD), dquery.reshape(tok_rows, 2 * HD)),
        )

    (key_total, value_total), (attended_parts, dquery_parts) = lax.scan(
        joint_step, (empty, empty), pair_ids
    )
    attended, d_query = (
        lax.all_to_all(
            merge_parts(attended_parts), "head", split_axis=0, concat_axis=1, tiled=True
        ),
        lax.all_to_all(merge_parts(dquery_parts), "head", split_axis=0, concat_axis=1, tiled=True),
    )
    from_upper = (
        passed_along(key_total[:span].astype(jnp.bfloat16), "ctx", -1).astype(jnp.float32),
        passed_along(value_total[:span].astype(jnp.bfloat16), "ctx", -1).astype(jnp.float32),
    )
    own_key = key_total[span:] + from_upper[0]
    own_value = value_total[span:] + from_upper[1]
    returned = (
        partner_2(own_key.astype(jnp.bfloat16), "ctx", 0).astype(own_key.dtype),
        partner_2(own_value.astype(jnp.bfloat16), "ctx", 0).astype(own_value.dtype),
    )
    d_keys = jnp.where(flipped, returned[0], own_key)
    d_values = jnp.where(flipped, returned[1], own_value)
    return (attended, d_query, d_keys, d_values)


def solution(mesh):
    placed = (
        P(("ctx", "head"), None),
        P(("ctx", "head"), None),
        P("ctx", "head"),
        P("ctx", "head"),
        P("ctx"),
        P(),
    )
    return jax.shard_map(
        per_device,
        mesh=mesh,
        in_specs=placed,
        out_specs=(
            P(("ctx", "head"), None),
            P(("ctx", "head"), None),
            P("ctx", "head"),
            P("ctx", "head"),
        ),
        check_vma=False,
    )
```

profile of v0, /device:TPU:56, one launch (start us, length us, event | category | flops | bytes accessed | tf_op | source)
XLA Modules:
  0.0 172.8 jit_solution(5823289868281014424)
XLA Ops:
  0.6 1.9 %copy.106 = bf16[4,8,8,1024]{3,2,0,1:T(8,128)(2,1)} copy(bf16[4,8,8,1024]{3,2,1,0:T(8,128)(2,1)} %bitcast.142) | data formatting | bytes 1048576 | tf_op jit(solution)/shard_map/all_to_all | solution.py:60
  2.6 6.3 %all-to-all-start = ((bf16[32,8,1024]{2,0,1:T(8,128)(2,1)}), bf16[32,8,1024]{2,0,1:T(8,128)(2,1)S(1)}, u32[]{:S(2)}, u32[]{:S(2)}) async-start(bf16[32,8,1024]{2,0,1:T(8,128)(2,1)} %bitcast.86), calls=%async_computation | async-start | bytes 1048576 | tf_op jit(solution)/shard_map/all_to_all | solution.py:60
  8.9 3.4 %collective-permute-start = (bf16[1024,128]{1,0:T(8,128)(2,1)}, bf16[1024,128]{1,0:T(8,128)(2,1)S(1)}, u32[]{:S(2)}, u32[]{:S(2)}) collective-permute-start(bf16[1024,128]{1,0:T(8,128)(2,1)} %param.10), channel_id=1, source_target_pairs={{0,8},{8,0},{16,24},{24,16},{32,40},{40,32},{48,56},{56,48},{64,72... | collective-permute-start | bytes 786440 | tf_op jit(solution)/shard_map/ppermute | solution.py:15
  12.3 2.4 %collective-permute-start.2 = (bf16[1024,128]{1,0:T(8,128)(2,1)}, bf16[1024,128]{1,0:T(8,128)(2,1)S(1)}, u32[]{:S(2)}, u32[]{:S(2)}) collective-permute-start(bf16[1024,128]{1,0:T(8,128)(2,1)} %param.11), channel_id=1, source_target_pairs={{0,8},{8,0},{16,24},{24,16},{32,40},{40,32},{48,56},{56,48},{64,72... | collective-permute-start | bytes 786440 | tf_op jit(solution)/shard_map/ppermute | solution.py:15
  17.3 1.9 %copy.105 = bf16[4,8,8,1024]{3,2,0,1:T(8,128)(2,1)} copy(bf16[4,8,8,1024]{3,2,1,0:T(8,128)(2,1)} %bitcast.143) | data formatting | bytes 1048576 | tf_op jit(solution)/shard_map/all_to_all | solution.py:61
  20.2 3.4 %collective-permute-start.1 = (bf16[1024,128]{1,0:T(8,128)(2,1)S(1)}, bf16[1024,128]{1,0:T(8,128)(2,1)}, u32[]{:S(2)}, u32[]{:S(2)}) collective-permute-start(bf16[1024,128]{1,0:T(8,128)(2,1)S(1)} %broadcast_select_fusion.1), channel_id=1, source_target_pairs={{0,8},{8,16},{16,24},{24,32},{32,40},{40,48},{48,56},{56,64},{64,7... | collective-permute-start | bytes 786440 | tf_op jit(solution)/shard_map/ppermute | solution.py:21
  23.6 5.1 %all-to-all-start.1 = ((bf16[32,8,1024]{2,0,1:T(8,128)(2,1)}), bf16[32,8,1024]{2,0,1:T(8,128)(2,1)}, u32[]{:S(2)}, u32[]{:S(2)}) async-start(bf16[32,8,1024]{2,0,1:T(8,128)(2,1)} %bitcast.85), calls=%async_computation.1 | async-start | bytes 1048576 | tf_op jit(solution)/shard_map/all_to_all | solution.py:61
  28.8 4.3 %collective-permute-start.3 = (bf16[1024,128]{1,0:T(8,128)(2,1)S(1)}, bf16[1024,128]{1,0:T(8,128)(2,1)}, u32[]{:S(2)}, u32[]{:S(2)}) collective-permute-start(bf16[1024,128]{1,0:T(8,128)(2,1)S(1)} %broadcast_select_fusion), channel_id=1, source_target_pairs={{0,8},{8,16},{16,24},{24,32},{32,40},{40,48},{48,56},{56,64},{64,7... | collective-permute-start | bytes 786440 | tf_op jit(solution)/shard_map/ppermute | solution.py:21
  34.3 5.4 %collective-permute-done.1 = bf16[1024,128]{1,0:T(8,128)(2,1)} collective-permute-done((bf16[1024,128]{1,0:T(8,128)(2,1)S(1)}, bf16[1024,128]{1,0:T(8,128)(2,1)}, u32[]{:S(2)}, u32[]{:S(2)}) %collective-permute-start.1) | collective-permute-done | bytes 262176 | tf_op jit(solution)/shard_map/ppermute | solution.py:21
  42.7 13.5 %collective-permute-done.3 = bf16[1024,128]{1,0:T(8,128)(2,1)} collective-permute-done((bf16[1024,128]{1,0:T(8,128)(2,1)S(1)}, bf16[1024,128]{1,0:T(8,128)(2,1)}, u32[]{:S(2)}, u32[]{:S(2)}) %collective-permute-start.3) | collective-permute-done | bytes 262176 | tf_op jit(solution)/shard_map/ppermute | solution.py:21
  58.0 2.0 %copy.82 = bf16[2048,128]{0,1:T(8,128)(2,1)} copy(bf16[2048,128]{1,0:T(8,128)(2,1)} %pad_maximum_fusion.1) | data formatting | bytes 1048576
  60.0 47.8 %while.19 = (s32[]{:T(128)}, f32[2048,128]{1,0:T(8,128)S(1)}, f32[2048,128]{1,0:T(8,128)S(1)}, bf16[4,256,256]{1,2,0:T(8,128)(2,1)}, bf16[4,256,256]{1,2,0:T(8,1...) while((s32[]{:T(128)}, f32[2048,128]{1,0:T(8,128)S(1)}, ...), condition=%wide.region_4.5_spmd.clone, body=%wide.region_0.4_spmd.clone.sunk | while | flops 1624966656 | bytes 47065372 | solution.py:112
  63.5 2.0 %fusion.63 = (f32[2,256]{1,0:T(2,128)S(1)}, f32[2,256,2048]{2,1,0:T(8,128)S(1)}) fusion(f32[256,2,2048]{2,0,1:T(8,128)S(1)} %fusion.62, pred[256,2048]{1,0:T(8,128)(4,1)S(1)} %copy-done), kind=kOutput, calls=%fused_computation.51.clone.1 | output fusion | flops 6293503 | bytes 8914944 | tf_op jit(solution)/shard_map/while/body/eval_jaxpr/sub | solution.py:30
  75.4 2.0 %fusion.63 = (f32[2,256]{1,0:T(2,128)S(1)}, f32[2,256,2048]{2,1,0:T(8,128)S(1)}) fusion(f32[256,2,2048]{2,0,1:T(8,128)S(1)} %fusion.62, pred[256,2048]{1,0:T(8,128)(4,1)S(1)} %copy-done), kind=kOutput, calls=%fused_computation.51.clone.1 | output fusion | flops 6293503 | bytes 8914944 | tf_op jit(solution)/shard_map/while/body/eval_jaxpr/sub | solution.py:30
  87.4 2.0 %fusion.63 = (f32[2,256]{1,0:T(2,128)S(1)}, f32[2,256,2048]{2,1,0:T(8,128)S(1)}) fusion(f32[256,2,2048]{2,0,1:T(8,128)S(1)} %fusion.62, pred[256,2048]{1,0:T(8,128)(4,1)S(1)} %copy-done), kind=kOutput, calls=%fused_computation.51.clone.1 | output fusion | flops 6293503 | bytes 8914944 | tf_op jit(solution)/shard_map/while/body/eval_jaxpr/sub | solution.py:30
  99.4 2.0 %fusion.63 = (f32[2,256]{1,0:T(2,128)S(1)}, f32[2,256,2048]{2,1,0:T(8,128)S(1)}) fusion(f32[256,2,2048]{2,0,1:T(8,128)S(1)} %fusion.62, pred[256,2048]{1,0:T(8,128)(4,1)S(1)} %copy-done), kind=kOutput, calls=%fused_computation.51.clone.1 | output fusion | flops 6293503 | bytes 8914944 | tf_op jit(solution)/shard_map/while/body/eval_jaxpr/sub | solution.py:30
  110.4 12.9 %all-to-all-start.2 = ((bf16[8,32,1024]{2,1,0:T(8,128)(2,1)}), bf16[8,32,1024]{2,1,0:T(8,128)(2,1)S(1)}, u32[]{:S(2)}, u32[]{:S(2)}) async-start(bf16[8,32,1024]{2,1,0:T(8,128)(2,1)} %all_to_all.64), calls=%async_computation.2 | async-start | bytes 1048576 | tf_op jit(solution)/shard_map/all_to_all | solution.py:116
  129.1 1.9 %collective-permute-start.4 = (bf16[1024,128]{1,0:T(8,128)(2,1)}, bf16[1024,128]{1,0:T(8,128)(2,1)}, u32[]{:S(2)}, u32[]{:S(2)}) collective-permute-start(bf16[1024,128]{1,0:T(8,128)(2,1)} %slice.33), channel_id=1, source_target_pairs={{8,0},{16,8},{24,16},{32,24},{40,32},{48,40},{56,48},{64,56},{72,6... | collective-permute-start | bytes 786440 | tf_op jit(solution)/shard_map/ppermute | solution.py:21
  131.0 16.3 %all-to-all-done.2 = bf16[8,32,1024]{2,1,0:T(8,128)(2,1)S(1)} async-done(((bf16[8,32,1024]{2,1,0:T(8,128)(2,1)}), bf16[8,32,1024]{2,1,0:T(8,128)(2,1)S(1)}, u32[]{:S(2)}, u32[]{:S(2)}) %all-to-all-start.2) | async-done | bytes 524320 | tf_op jit(solution)/shard_map/all_to_all | solution.py:116
  147.3 6.1 %all-to-all-start.3 = ((bf16[8,32,1024]{2,1,0:T(8,128)(2,1)}), bf16[8,32,1024]{2,1,0:T(8,128)(2,1)S(1)}, u32[]{:S(2)}, u32[]{:S(2)}) async-start(bf16[8,32,1024]{2,1,0:T(8,128)(2,1)} %all_to_all.68), calls=%async_computation.3 | async-start | bytes 1048576 | tf_op jit(solution)/shard_map/all_to_all | solution.py:119
  153.4 1.9 %collective-permute-start.7 = (bf16[1024,128]{1,0:T(8,128)(2,1)S(1)}, bf16[1024,128]{1,0:T(8,128)(2,1)S(1)}, u32[]{:S(2)}, u32[]{:S(2)}) collective-permute-start(bf16[1024,128]{1,0:T(8,128)(2,1)S(1)} %fusion.23), channel_id=1, source_target_pairs={{0,8},{8,0},{16,24},{24,16},{32,40},{40,32},{48,56},{56,48},{64,72... | collective-permute-start | bytes 786440 | tf_op jit(solution)/shard_map/ppermute | solution.py:15
  156.4 3.9 %collective-permute-start.5 = (bf16[1024,128]{1,0:T(8,128)(2,1)S(1)}, bf16[1024,128]{1,0:T(8,128)(2,1)S(1)}, u32[]{:S(2)}, u32[]{:S(2)}) collective-permute-start(bf16[1024,128]{1,0:T(8,128)(2,1)S(1)} %fusion.22), channel_id=1, source_target_pairs={{0,8},{8,0},{16,24},{24,16},{32,40},{40,32},{48,56},{56,48},{64,72... | collective-permute-start | bytes 786440 | tf_op jit(solution)/shard_map/ppermute | solution.py:15
  160.3 4.2 %collective-permute-done.7 = bf16[1024,128]{1,0:T(8,128)(2,1)S(1)} collective-permute-done((bf16[1024,128]{1,0:T(8,128)(2,1)S(1)}, bf16[1024,128]{1,0:T(8,128)(2,1)S(1)}, u32[]{:S(2)}, u32[]{:S(2)}) %collective-permute-start.7) | collective-permute-done | bytes 262176 | tf_op jit(solution)/shard_map/ppermute | solution.py:15
  165.3 4.0 %collective-permute-done.5 = bf16[1024,128]{1,0:T(8,128)(2,1)S(1)} collective-permute-done((bf16[1024,128]{1,0:T(8,128)(2,1)S(1)}, bf16[1024,128]{1,0:T(8,128)(2,1)S(1)}, u32[]{:S(2)}, u32[]{:S(2)}) %collective-permute-start.5) | collective-permute-done | bytes 262176 | tf_op jit(solution)/shard_map/ppermute | solution.py:15
  (105 shorter events, 59.4 us)
Async XLA Ops:
  0.6 28.1 %copy-start.2 = (bf16[1024,128]{1,0:T(8,128)(2,1)S(1)}, bf16[1024,128]{1,0:T(8,128)(2,1)}, u32[]{:S(2)}) copy-start(bf16[1024,128]{1,0:T(8,128)(2,1)} %param.11) | copy-start | bytes 786436
  2.6 21.0 %all-to-all-start = ((bf16[32,8,1024]{2,0,1:T(8,128)(2,1)}), bf16[32,8,1024]{2,0,1:T(8,128)(2,1)S(1)}, u32[]{:S(2)}, u32[]{:S(2)}) async-start(bf16[32,8,1024]{2,0,1:T(8,128)(2,1)} %bitcast.86), calls=%async_computation | async-start | bytes 1048576 | tf_op jit(solution)/shard_map/all_to_all | solution.py:60
  8.9 11.2 %collective-permute-start = (bf16[1024,128]{1,0:T(8,128)(2,1)}, bf16[1024,128]{1,0:T(8,128)(2,1)S(1)}, u32[]{:S(2)}, u32[]{:S(2)}) collective-permute-start(bf16[1024,128]{1,0:T(8,128)(2,1)} %param.10), channel_id=1, source_target_pairs={{0,8},{8,0},{16,24},{24,16},{32,40},{40,32},{48,56},{56,48},{64,72... | collective-permute-start | bytes 786440 | tf_op jit(solution)/shard_map/ppermute | solution.py:15
  12.3 16.4 %collective-permute-start.2 = (bf16[1024,128]{1,0:T(8,128)(2,1)}, bf16[1024,128]{1,0:T(8,128)(2,1)S(1)}, u32[]{:S(2)}, u32[]{:S(2)}) collective-permute-start(bf16[1024,128]{1,0:T(8,128)(2,1)} %param.11), channel_id=1, source_target_pairs={{0,8},{8,0},{16,24},{24,16},{32,40},{40,32},{48,56},{56,48},{64,72... | collective-permute-start | bytes 786440 | tf_op jit(solution)/shard_map/ppermute | solution.py:15
  20.2 19.5 %collective-permute-start.1 = (bf16[1024,128]{1,0:T(8,128)(2,1)S(1)}, bf16[1024,128]{1,0:T(8,128)(2,1)}, u32[]{:S(2)}, u32[]{:S(2)}) collective-permute-start(bf16[1024,128]{1,0:T(8,128)(2,1)S(1)} %broadcast_select_fusion.1), channel_id=1, source_target_pairs={{0,8},{8,16},{16,24},{24,32},{32,40},{40,48},{48,56},{56,64},{64,7... | collective-permute-start | bytes 786440 | tf_op jit(solution)/shard_map/ppermute | solution.py:21
  23.6 36.4 %all-to-all-start.1 = ((bf16[32,8,1024]{2,0,1:T(8,128)(2,1)}), bf16[32,8,1024]{2,0,1:T(8,128)(2,1)}, u32[]{:S(2)}, u32[]{:S(2)}) async-start(bf16[32,8,1024]{2,0,1:T(8,128)(2,1)} %bitcast.85), calls=%async_computation.1 | async-start | bytes 1048576 | tf_op jit(solution)/shard_map/all_to_all | solution.py:61
  28.8 27.4 %collective-permute-start.3 = (bf16[1024,128]{1,0:T(8,128)(2,1)S(1)}, bf16[1024,128]{1,0:T(8,128)(2,1)}, u32[]{:S(2)}, u32[]{:S(2)}) collective-permute-start(bf16[1024,128]{1,0:T(8,128)(2,1)S(1)} %broadcast_select_fusion), channel_id=1, source_target_pairs={{0,8},{8,16},{16,24},{24,32},{32,40},{40,48},{48,56},{56,64},{64,7... | collective-permute-start | bytes 786440 | tf_op jit(solution)/shard_map/ppermute | solution.py:21
  62.4 1.0 copy-start
  65.5 1.0 copy-start.1
  74.4 1.0 copy-start
  77.5 1.0 copy-start.1
  86.4 1.0 copy-start
  89.4 1.0 copy-start.1
  98.3 1.0 copy-start
  101.4 1.0 copy-start.1
  110.4 36.9 %all-to-all-start.2 = ((bf16[8,32,1024]{2,1,0:T(8,128)(2,1)}), bf16[8,32,1024]{2,1,0:T(8,128)(2,1)S(1)}, u32[]{:S(2)}, u32[]{:S(2)}) async-start(bf16[8,32,1024]{2,1,0:T(8,128)(2,1)} %all_to_all.64), calls=%async_computation.2 | async-start | bytes 1048576 | tf_op jit(solution)/shard_map/all_to_all | solution.py:116
  124.0 29.4 %collective-permute-start.6 = (bf16[1024,128]{1,0:T(8,128)(2,1)}, bf16[1024,128]{1,0:T(8,128)(2,1)S(1)}, u32[]{:S(2)}, u32[]{:S(2)}) collective-permute-start(bf16[1024,128]{1,0:T(8,128)(2,1)} %slice.32), channel_id=1, source_target_pairs={{8,0},{16,8},{24,16},{32,24},{40,32},{48,40},{56,48},{64,56},{72,6... | collective-permute-start | bytes 786440 | tf_op jit(solution)/shard_map/ppermute | solution.py:21
  129.1 26.2 %collective-permute-start.4 = (bf16[1024,128]{1,0:T(8,128)(2,1)}, bf16[1024,128]{1,0:T(8,128)(2,1)}, u32[]{:S(2)}, u32[]{:S(2)}) collective-permute-start(bf16[1024,128]{1,0:T(8,128)(2,1)} %slice.33), channel_id=1, source_target_pairs={{8,0},{16,8},{24,16},{32,24},{40,32},{48,40},{56,48},{64,56},{72,6... | collective-permute-start | bytes 786440 | tf_op jit(solution)/shard_map/ppermute | solution.py:21
  147.3 24.7 %all-to-all-start.3 = ((bf16[8,32,1024]{2,1,0:T(8,128)(2,1)}), bf16[8,32,1024]{2,1,0:T(8,128)(2,1)S(1)}, u32[]{:S(2)}, u32[]{:S(2)}) async-start(bf16[8,32,1024]{2,1,0:T(8,128)(2,1)} %all_to_all.68), calls=%async_computation.3 | async-start | bytes 1048576 | tf_op jit(solution)/shard_map/all_to_all | solution.py:119
  153.4 11.0 %collective-permute-start.7 = (bf16[1024,128]{1,0:T(8,128)(2,1)S(1)}, bf16[1024,128]{1,0:T(8,128)(2,1)S(1)}, u32[]{:S(2)}, u32[]{:S(2)}) collective-permute-start(bf16[1024,128]{1,0:T(8,128)(2,1)S(1)} %fusion.23), channel_id=1, source_target_pairs={{0,8},{8,0},{16,24},{24,16},{32,40},{40,32},{48,56},{56,48},{64,72... | collective-permute-start | bytes 786440 | tf_op jit(solution)/shard_map/ppermute | solution.py:15
  156.4 12.9 %collective-permute-start.5 = (bf16[1024,128]{1,0:T(8,128)(2,1)S(1)}, bf16[1024,128]{1,0:T(8,128)(2,1)S(1)}, u32[]{:S(2)}, u32[]{:S(2)}) collective-permute-start(bf16[1024,128]{1,0:T(8,128)(2,1)S(1)} %fusion.22), channel_id=1, source_target_pairs={{0,8},{8,0},{16,24},{24,16},{32,40},{40,32},{48,56},{56,48},{64,72... | collective-permute-start | bytes 786440 | tf_op jit(solution)/shard_map/ppermute | solution.py:15
where the time goes:
time: 175 us; the launch traced here: 173 us
  starting transfers between devices  53.6 us (31%)
  waiting for transfers between devices  44.2 us (25%)
  local copies, waits for them, and re-layouts  29.4 us (17%)
  matrix products  21.5 us (12%)
  other arithmetic  19.7 us (11%)
  loops' own time  2.95 us (2%)
    ppermute x4, waiting for transfers between devices, passed_along(): return lax.ppermute(value, axis, pairs)  18.9 us
    all_to_all x1, waiting for transfers between devices, per_device(): lax.all_to_all(merge_parts(attended_parts), 'head', split_axis=0, concat_...  16.3 us
    all_to_all x1, starting transfers between devices, per_device(): lax.all_to_all(merge_parts(attended_parts), 'head', split_axis=0, concat_...  12.9 us
    ppermute x4, starting transfers between devices, partner_2(): lax.ppermute(value, axis, [(i, i ^ 1 << apart) for i in range(lax.axis_si...  11.7 us
    ppermute x4, starting transfers between devices, passed_along(): return lax.ppermute(value, axis, pairs)  11.6 us
    ppermute x4, waiting for transfers between devices, partner_2(): lax.ppermute(value, axis, [(i, i ^ 1 << apart) for i in range(lax.axis_si...  9.02 us
    sub x4, other arithmetic, pair_weights(): expo = jnp.exp(scores - top)  8.17 us
    all_to_all x1, starting transfers between devices, per_device(): lax.all_to_all(query, 'head', split_axis=1, concat_axis=0, tiled=True)  6.35 us
  transfers between devices with their start and end apart: 12, of which 6 were waited for; matrix products, arithmetic and copies ran while one was open for 11% of the time, Pallas kernels for 0%

commit v1 on v0

v1 whole, which is shorter than its diff:
```python
import functools

import jax
import jax.numpy as jnp
from jax import lax
from jax.experimental import pallas as pl
from jax.experimental.pallas import tpu as pltpu
from jax.sharding import PartitionSpec as P

HD = 128
GROUP = 8
COLS = GROUP * HD
ROWS = 1024
PIECE = 256
PIECES = ROWS // PIECE
FACTOR = HD**-0.5
LOG2E = 1.4426950408889634
MESH = pl.DeviceIdType.MESH
BF16 = jnp.bfloat16
F32 = jnp.float32


def half(x, n):
    return lax.rem(x, n)


def peer_of(h, r):
    b0 = lax.rem(h + r, 2)
    b1 = lax.rem(lax.div(h, 2) + lax.div(r, 2), 2)
    b2 = lax.rem(lax.div(h, 4) + lax.div(r, 4), 2)
    return b0 + 2 * b1 + 4 * b2


def stacked(tile):
    return jnp.concatenate([tile[:, j * HD : (j + 1) * HD] for j in range(GROUP)], axis=0)


def unstacked(rows, toks):
    return jnp.concatenate([rows[j * toks : (j + 1) * toks] for j in range(GROUP)], axis=1)


def tile_step(q_tile, g_tile, first_tok, n_low, kk, vv, kkt, vvt, dkk, dvv):
    toks = q_tile.shape[0]
    rows = toks * GROUP
    q2 = stacked(q_tile).astype(F32)
    g2 = stacked(g_tile).astype(F32)
    tok_row = lax.rem(lax.broadcasted_iota(jnp.int32, (rows, HD), 0), toks) + first_tok
    low_row = tok_row < n_low
    tok_lane = lax.rem(lax.broadcasted_iota(jnp.int32, (HD, rows), 1), toks) + first_tok
    low_lane = tok_lane < n_low
    zero = jnp.zeros((rows, HD), F32)
    zero_t = jnp.zeros((HD, rows), F32)
    qt = jnp.transpose(q2)
    gt = jnp.transpose(g2)
    qq = jnp.concatenate([jnp.where(low_row, q2, zero), jnp.where(low_row, zero, q2)], axis=1).astype(BF16)
    gg = jnp.concatenate([jnp.where(low_row, g2, zero), jnp.where(low_row, zero, g2)], axis=1).astype(BF16)
    qqt = jnp.concatenate([jnp.where(low_lane, qt, zero_t), jnp.where(low_lane, zero_t, qt)], axis=0).astype(BF16)
    ggt = jnp.concatenate([jnp.where(low_lane, gt, zero_t), jnp.where(low_lane, zero_t, gt)], axis=0).astype(BF16)
    st = jnp.dot(kk[...], qqt, preferred_element_type=F32)
    top = jnp.max(st, axis=0, keepdims=True)
    ex = jnp.exp2((st - top) * (FACTOR * LOG2E))
    inv = 1.0 / jnp.sum(ex, axis=0, keepdims=True)
    w = ex * inv
    p = w.astype(BF16)
    ot = jnp.dot(vvt[...], p, preferred_element_type=F32)
    ot = jnp.where(low_lane, ot[:HD], ot[HD:]).astype(BF16).astype(F32)
    delta = jnp.sum(gt * ot, axis=0, keepdims=True)
    dp = jnp.dot(vv[...], ggt, preferred_element_type=F32)
    ds = (w * (dp - delta)).astype(BF16)
    dvv[...] += jnp.dot(p, gg, preferred_element_type=F32)
    dkk[...] += jnp.dot(ds, qq, preferred_element_type=F32)
    dqt = jnp.dot(kkt[...], ds, preferred_element_type=F32)
    dqt = jnp.where(low_lane, dqt[:HD], dqt[HD:]) * FACTOR
    att = unstacked(jnp.transpose(ot).astype(BF16), toks)
    dq = unstacked(jnp.transpose(dqt).astype(BF16), toks)
    return att, dq


def kernel(
    n_ctx,
    q_ref,
    g_ref,
    k_ref,
    v_ref,
    img_ref,
    owner_ref,
    att_ref,
    dq_ref,
    dk_ref,
    dv_ref,
    qb,
    gb,
    ob,
    db,
    own,
    part,
    low,
    fwd,
    kk,
    vv,
    kkt,
    vvt,
    dkk,
    dvv,
    part_g,
    prev_g,
    part_in,
    next_in,
    fin,
    own_sem,
    in_send,
    in_recv,
    out_send,
    out_recv,
    part_send,
    part_recv,
    fwd_send,
    fwd_recv,
    pg_send,
    pg_recv,
    ng_send,
    ng_recv,
    loc_sem,
):
    c = lax.axis_index("ctx")
    h = lax.axis_index("head")
    toks = qb.shape[1]
    odd = lax.rem(c, 2) == 1
    even = lax.rem(c, 2) == 0
    mate = c + 1 - 2 * lax.rem(c, 2)
    side = lax.rem(c + 2 * lax.rem(c, 2) - 1 + n_ctx, n_ctx)
    has_side = jnp.logical_and(c > 0, c < n_ctx - 1)
    gives = jnp.logical_and(odd, c < n_ctx - 1)
    takes = jnp.logical_and(even, c > 0)

    def cols(p):
        return pl.ds(pl.multiple_of(p * COLS, COLS), COLS)

    def piece(i):
        return lax.div(i, PIECES), pl.ds(pl.multiple_of(lax.rem(i, PIECES) * PIECE, PIECE), PIECE)

    def remote(src, dst, send, recv, place, head):
        return pltpu.make_async_remote_copy(
            src_ref=src, dst_ref=dst, send_sem=send, recv_sem=recv, device_id=(place, head), device_id_type=MESH
        )

    def mate_copy(i, src, dst, send, recv):
        a, rows = piece(i)
        return remote(src.at[a, rows], dst.at[a, rows], send.at[i], recv.at[i], mate, h)

    def side_copy(i, src, dst, send, recv):
        a, rows = piece(i)
        return remote(src.at[a, rows], dst.at[a, rows], send.at[i], recv.at[i], side, h)

    def in_copy(k, r):
        src, dst = ((q_ref, qb), (g_ref, gb))[k]
        p = peer_of(h, r)
        return remote(src.at[:, cols(p)], dst.at[r], in_send.at[k, r], in_recv.at[k, r], c, p)

    def out_copy(k, r):
        src, dst = ((ob, att_ref), (db, dq_ref))[k]
        p = peer_of(h, r)
        return remote(src.at[r], dst.at[:, cols(h)], out_send.at[k, r], out_recv.at[k, r], c, p)

    barrier = pltpu.get_barrier_semaphore()
    for r in range(1, 8):
        pl.semaphore_signal(barrier, inc=1, device_id=(c, peer_of(h, r)), device_id_type=MESH)
    pl.semaphore_signal(barrier, inc=1, device_id=(mate, h), device_id_type=MESH)

    own_copies = [pltpu.make_async_copy(ref, own.at[a], own_sem.at[a]) for a, ref in enumerate((k_ref, v_ref))]
    own_tiles = [
        pltpu.make_async_copy(ref.at[:, cols(h)], buf.at[0], own_sem.at[2 + a])
        for a, (ref, buf) in enumerate(((q_ref, qb), (g_ref, gb)))
    ]
    for copy in own_copies + own_tiles:
        copy.start()

    @pl.when(has_side)
    def _():
        pl.semaphore_signal(barrier, inc=1, device_id=(side, h), device_id_type=MESH)
        pl.semaphore_wait(barrier, 9)

    @pl.when(jnp.logical_not(has_side))
    def _():
        pl.semaphore_wait(barrier, 8)

    for copy in own_copies:
        copy.wait()

    def send_own(i, carry):
        mate_copy(i, own, part, part_send, part_recv).start()
        return carry

    lax.fori_loop(0, 2 * PIECES, send_own, 0)

    def send_in(i, carry):
        for k in range(2):
            in_copy(k, 8 - i).start()
        return carry

    lax.fori_loop(1, 8, send_in, 0)

    dkk[...] = jnp.zeros_like(dkk)
    dvv[...] = jnp.zeros_like(dvv)

    flip_all = jnp.full((PIECE, HD), owner_ref[c], jnp.int32) != c
    n_low = jnp.sum((img_ref[...] < c).astype(jnp.int32), axis=1, keepdims=True)

    @pl.when(odd)
    def _():
        def take(i, carry):
            a, rows = piece(i)
            mate_copy(i, own, part, part_send, part_recv).wait_recv()
            mine = own[a, rows].astype(F32)
            other = part[a, rows].astype(F32)
            fwd[a, rows] = jnp.where(flip_all, other, mine).astype(BF16)
            low[a, rows] = jnp.where(flip_all, mine, other).astype(BF16)

            @pl.when(gives)
            def _():
                side_copy(i, fwd, low, fwd_send, fwd_recv).start()

            return carry

        lax.fori_loop(0, 2 * PIECES, take, 0)

    @pl.when(even)
    def _():
        def take(i, carry):
            a, rows = piece(i)
            mate_copy(i, own, part, part_send, part_recv).wait_recv()
            mine = own[a, rows].astype(F32)
            other = part[a, rows].astype(F32)
            fwd[a, rows] = jnp.where(flip_all, other, mine).astype(BF16)
            return carry

        lax.fori_loop(0, 2 * PIECES, take, 0)

        @pl.when(takes)
        def _():
            def arrive(i, carry):
                side_copy(i, fwd, low, fwd_send, fwd_recv).wait_recv()
                return carry

            lax.fori_loop(0, 2 * PIECES, arrive, 0)

        @pl.when(jnp.logical_not(takes))
        def _():
            low[...] = jnp.zeros_like(low)

    for a, (both, both_t) in enumerate(((kk, kkt), (vv, vvt))):
        both[:, :HD] = low[a]
        both[:, HD:] = fwd[a]
        both_t[:HD] = jnp.transpose(low[a].astype(F32)).astype(BF16)
        both_t[HD:] = jnp.transpose(fwd[a].astype(F32)).astype(BF16)

    def step(i, carry):
        r = lax.rem(8 - i, 8)

        @pl.when(r == 0)
        def _():
            for copy in own_tiles:
                copy.wait()

        @pl.when(r > 0)
        def _():
            for k in range(2):
                in_copy(k, r).wait_recv()

        att, dq = tile_step(qb[r], gb[r], peer_of(h, r) * toks, n_low, kk, vv, kkt, vvt, dkk, dvv)
        ob[r] = att
        db[r] = dq

        @pl.when(r == 0)
        def _():
            for a, (buf, ref) in enumerate(((ob, att_ref), (db, dq_ref))):
                pltpu.make_async_copy(buf.at[0], ref.at[:, cols(h)], loc_sem.at[a]).start()

        @pl.when(r > 0)
        def _():
            for k in range(2):
                out_copy(k, r).start()

        return carry

    lax.fori_loop(0, 8, step, 0)

    def summed(i):
        a, rows = piece(i)
        pick = jnp.full((PIECE, 2 * HD), a, jnp.int32) == 0
        both = jnp.where(pick, dkk[rows] * FACTOR, dvv[rows])
        return both[:, :HD], both[:, HD:]

    def put_out(i, value):
        a, rows = piece(i)
        fin[a, rows] = value

    @pl.when(even)
    def _():
        def give(i, carry):
            a, rows = piece(i)
            lower, upper = summed(i)
            prev_g[a, rows] = lower.astype(BF16)

            @pl.when(takes)
            def _():
                side_copy(i, prev_g, next_in, ng_send, ng_recv).start()

            part_g[a, rows] = upper.astype(BF16)
            mate_copy(i, part_g, part_in, pg_send, pg_recv).start()
            return carry

        lax.fori_loop(0, 2 * PIECES, give, 0)

        def finish(i, carry):
            a, rows = piece(i)
            mate_copy(i, part_g, part_in, pg_send, pg_recv).wait_recv()
            _, upper = summed(i)
            other = part_in[a, rows].astype(F32)
            put_out(i, jnp.where(flip_all, other, upper + other))
            return carry

        lax.fori_loop(0, 2 * PIECES, finish, 0)

    @pl.when(odd)
    def _():
        @pl.when(jnp.logical_not(gives))
        def _():
            next_in[...] = jnp.zeros_like(next_in)

        def finish(i, carry):
            a, rows = piece(i)

            @pl.when(gives)
            def _():
                side_copy(i, prev_g, next_in, ng_send, ng_recv).wait_recv()

            lower, upper = summed(i)
            upper = upper + next_in[a, rows].astype(F32)
            part_g[a, rows] = jnp.where(flip_all, upper, lower).astype(BF16)
            mate_copy(i, part_g, part_in, pg_send, pg_recv).start()
            mate_copy(i, part_g, part_in, pg_send, pg_recv).wait_recv()
            other = part_in[a, rows].astype(F32)
            put_out(i, jnp.where(flip_all, lower + other, upper))
            return carry

        lax.fori_loop(0, 2 * PIECES, finish, 0)

    outs = [pltpu.make_async_copy(fin.at[a], ref, loc_sem.at[2 + a]) for a, ref in enumerate((dk_ref, dv_ref))]
    for copy in outs:
        copy.start()

    def drain(i, carry):
        for k in range(2):
            in_copy(k, i).wait_send()
            out_copy(k, i).wait()
        return carry

    lax.fori_loop(1, 8, drain, 0)

    def drain_pieces(i, carry):
        mate_copy(i, own, part, part_send, part_recv).wait_send()
        mate_copy(i, part_g, part_in, pg_send, pg_recv).wait_send()

        @pl.when(gives)
        def _():
            side_copy(i, fwd, low, fwd_send, fwd_recv).wait_send()

        @pl.when(takes)
        def _():
            side_copy(i, prev_g, next_in, ng_send, ng_recv).wait_send()

        return carry

    lax.fori_loop(0, 2 * PIECES, drain_pieces, 0)
    for a, (buf, ref) in enumerate(((ob, att_ref), (db, dq_ref))):
        pltpu.make_async_copy(buf.at[0], ref.at[:, cols(h)], loc_sem.at[a]).wait()
    for copy in outs:
        copy.wait()


def per_device(n_ctx, query, d_out, keys_img, values_img, image_of, owner):
    toks = query.shape[0]
    anywhere = pl.BlockSpec(memory_space=pl.ANY)
    tile = pltpu.VMEM((8, toks, COLS), BF16)
    pair = pltpu.VMEM((2, ROWS, HD), BF16)
    dma = pltpu.SemaphoreType.DMA
    n = 2 * PIECES
    return pl.pallas_call(
        functools.partial(kernel, n_ctx),
        out_shape=(
            jax.ShapeDtypeStruct(query.shape, BF16),
            jax.ShapeDtypeStruct(query.shape, BF16),
            jax.ShapeDtypeStruct(keys_img.shape, F32),
            jax.ShapeDtypeStruct(values_img.shape, F32),
        ),
        in_specs=[anywhere] * 4
        + [pl.BlockSpec(memory_space=pltpu.VMEM), pl.BlockSpec(memory_space=pltpu.SMEM)],
        out_specs=(anywhere,) * 4,
        scratch_shapes=[tile] * 4
        + [pair] * 4
        + [pltpu.VMEM((ROWS, 2 * HD), BF16)] * 2
        + [pltpu.VMEM((2 * HD, ROWS), BF16)] * 2
        + [pltpu.VMEM((ROWS, 2 * HD), F32)] * 2
        + [pair] * 4
        + [pltpu.VMEM((2, ROWS, HD), F32)]
        + [dma((4,))]
        + [dma((2, 8))] * 4
        + [dma((n,))] * 8
        + [dma((4,))],
        compiler_params=pltpu.CompilerParams(collective_id=0, has_side_effects=True, vmem_limit_bytes=56 << 20),
        name="attend",
    )(query, d_out, keys_img, values_img, image_of.reshape(1, -1), owner)


def solution(mesh):
    placed = (
        P(("ctx", "head"), None),
        P(("ctx", "head"), None),
        P("ctx", "head"),
        P("ctx", "head"),
        P("ctx"),
        P(),
    )
    return jax.shard_map(
        functools.partial(per_device, mesh.shape["ctx"]),
        mesh=mesh,
        in_specs=placed,
        out_specs=(
            P(("ctx", "head"), None),
            P(("ctx", "head"), None),
            P("ctx", "head"),
            P("ctx", "head"),
        ),
        check_vma=False,
    )
```

time: 175 us -> 112 us (0.64)
  the two profiles are of different devices: /device:TPU:56 before, /device:TPU:468 now
where the time goes in v1:
time: 112 us
  Pallas kernels  106 us (95%)
  local copies, waits for them, and re-layouts  5.18 us (5%)
    pallas_call x1, Pallas kernels, per_device(): pl.pallas_call(functools.partial(kernel, n_ctx), out_shape=(jax.ShapeDtyp...  106 us
    unnamed x10, local copies, waits for them, and re-layouts  5.18 us

profile of v1, /device:TPU:468, one launch (start us, length us, event | category | flops | bytes accessed | tf_op | source)
XLA Modules:
  0.0 111.8 jit_solution(7423019128179361277)
XLA Ops:
  0.6 106.0 %attend.1 = (bf16[32,8192]{1,0:T(8,128)(2,1)}, bf16[32,8192]{1,0:T(8,128)(2,1)}, f32[1024,128]{1,0:T(8,128)}, f32[1024,128]{1,0:T(8,128)}) custom-call(bf16[32,8192]{1,0:T(8,128)(2,1)} %q_ref.1, bf16[32,8192]{1,0:T(8,128)(2,1)} %g_ref.1, bf16[1024,128]{1,0:T(8,128)(2,1)} %k_ref.1, bf16[1024,128]{1,0:T(8,128)(2,1)} %v_ref.1, s32[1,256]{1,0:T(1,128)} %bitcast.1, ...), custom_call_target="tpu_custom_call" | custom-call | tf_op jit(solution)/shard_map/attend/pallas_call | solution.py:389
  106.6 0.0 copy-start.2
  106.7 1.9 %copy.14 = bf16[32,8192]{1,0:T(8,128)(2,1)} copy(bf16[32,8192]{1,0:T(8,128)(2,1)} %get-tuple-element.8) | data formatting | bytes 1048576
  108.6 0.0 copy-done.2
  108.6 0.0 copy-start.1
  108.6 0.8 copy.15
  109.4 0.4 copy-done.1
  109.8 0.0 copy-start
  109.8 0.8 copy.16
  110.6 0.4 copy-done
  111.0 0.8 copy.17
Async XLA Ops:
  106.6 1.9 %copy-start.2 = (bf16[32,8192]{1,0:T(8,128)(2,1)S(1)}, bf16[32,8192]{1,0:T(8,128)(2,1)}, u32[]{:S(2)}) copy-start(bf16[32,8192]{1,0:T(8,128)(2,1)} %get-tuple-element.9) | copy-start | bytes 1572868
  108.6 1.2 %copy-start.1 = (f32[1024,128]{1,0:T(8,128)S(1)}, f32[1024,128]{1,0:T(8,128)}, u32[]{:S(2)}) copy-start(f32[1024,128]{1,0:T(8,128)} %get-tuple-element.10) | copy-start | bytes 1572868
  109.8 1.2 %copy-start = (f32[1024,128]{1,0:T(8,128)S(1)}, f32[1024,128]{1,0:T(8,128)}, u32[]{:S(2)}) copy-start(f32[1024,128]{1,0:T(8,128)} %get-tuple-element.11) | copy-start | bytes 1572868

commit v2 on v1

v2 whole, which is shorter than its diff:
```python
import functools

import jax
import jax.numpy as jnp
from jax import lax
from jax.experimental import pallas as pl
from jax.experimental.pallas import tpu as pltpu
from jax.sharding import PartitionSpec as P

HD = 128
GROUP = 8
COLS = GROUP * HD
ROWS = 1024
PIECE = 256
PIECES = ROWS // PIECE
N = 2 * PIECES
FACTOR = HD**-0.5
LOG2E = 1.4426950408889634
LATE, RELAY = 5, 5
MESH = pl.DeviceIdType.MESH
BF16 = jnp.bfloat16
F32 = jnp.float32


def peer_of(h, r):
    b0 = lax.rem(h + r, 2)
    b1 = lax.rem(lax.div(h, 2) + lax.div(r, 2), 2)
    b2 = lax.rem(lax.div(h, 4) + lax.div(r, 4), 2)
    return b0 + 2 * b1 + 4 * b2


def stacked(tile):
    return jnp.concatenate([tile[:, j * HD : (j + 1) * HD] for j in range(GROUP)], axis=0)


def unstacked(rows, toks):
    return jnp.concatenate([rows[j * toks : (j + 1) * toks] for j in range(GROUP)], axis=1)


def pair_step(q_tiles, g_tiles, firsts, n_low, kk, vv, kkt, vvt, p_ref, ds_ref, qs_ref, gs_ref):
    toks = q_tiles[0].shape[0]
    each = toks * GROUP
    rows = 2 * each
    q2 = jnp.concatenate([stacked(tile) for tile in q_tiles], axis=0).astype(F32)
    g2 = jnp.concatenate([stacked(tile) for tile in g_tiles], axis=0).astype(F32)

    def is_low(shape, axis):
        at = lax.broadcasted_iota(jnp.int32, shape, axis)
        return lax.rem(at, toks) + jnp.where(at < each, firsts[0], firsts[1]) < n_low

    low_lane = is_low((HD, rows), 1)
    low_row = is_low((rows, HD), 0)

    def halves(x, mask, axis):
        zero = jnp.zeros_like(x)
        return jnp.concatenate([jnp.where(mask, x, zero), jnp.where(mask, zero, x)], axis=axis).astype(BF16)

    qt = jnp.transpose(q2)
    gt = jnp.transpose(g2)
    st = jnp.dot(kk[...], halves(qt, low_lane, 0), preferred_element_type=F32)
    top = jnp.max(st, axis=0, keepdims=True)
    ex = jnp.exp2((st - top) * (FACTOR * LOG2E))
    inv = 1.0 / jnp.sum(ex, axis=0, keepdims=True)
    p = ex.astype(BF16)
    p_ref[...] = p
    inv_row = jnp.transpose(jnp.broadcast_to(inv, (HD, rows)))
    qs_ref[...] = halves(q2 * inv_row, low_row, 1)
    gs_ref[...] = halves(g2 * inv_row, low_row, 1)
    ot = jnp.dot(vvt[...], p, preferred_element_type=F32)
    ot = (jnp.where(low_lane, ot[:HD], ot[HD:]) * inv).astype(BF16).astype(F32)
    delta = jnp.sum(gt * ot, axis=0, keepdims=True)
    dp = jnp.dot(vv[...], halves(gt, low_lane, 0), preferred_element_type=F32)
    ds = (p.astype(F32) * (dp - delta)).astype(BF16)
    ds_ref[...] = ds
    dqt = jnp.dot(kkt[...], ds, preferred_element_type=F32)
    dqt = jnp.where(low_lane, dqt[:HD], dqt[HD:]) * (inv * FACTOR)
    att = jnp.transpose(ot).astype(BF16)
    dq = jnp.transpose(dqt).astype(BF16)
    return (
        [unstacked(att[:each], toks), unstacked(att[each:], toks)],
        [unstacked(dq[:each], toks), unstacked(dq[each:], toks)],
    )


def summed(left, right, rows):
    total = jnp.dot(left[0, rows], right[0], preferred_element_type=F32)
    for t in range(1, left.shape[0]):
        total = total + jnp.dot(left[t, rows], right[t], preferred_element_type=F32)
    return total


def kernel(
    n_ctx,
    q_ref,
    g_ref,
    k_ref,
    v_ref,
    img_ref,
    owner_ref,
    att_ref,
    dq_ref,
    dk_ref,
    dv_ref,
    qb,
    gb,
    ob,
    db,
    own,
    part,
    low,
    fwd,
    kk,
    vv,
    kkt,
    vvt,
    ps,
    dss,
    qs,
    gs,
    part_g,
    prev_g,
    part_in,
    next_in,
    fin,
    tot,
    own_sem,
    in_send,
    in_recv,
    out_send,
    out_recv,
    part_send,
    part_recv,
    fwd_send,
    fwd_recv,
    pg_send,
    pg_recv,
    ng_send,
    ng_recv,
    loc_sem,
    hop,
    hop_g,
    cand,
    hop_send,
    hop_recv,
    cand_recv,
    src_send,
):
    c = lax.axis_index("ctx")
    h = lax.axis_index("head")
    toks = qb.shape[1]
    odd = lax.rem(c, 2) == 1
    even = lax.rem(c, 2) == 0
    mate = c + 1 - 2 * lax.rem(c, 2)
    side = lax.rem(c + 2 * lax.rem(c, 2) - 1 + n_ctx, n_ctx)
    has_side = jnp.logical_and(c > 0, c < n_ctx - 1)
    mid = n_ctx // 2
    subs = mid // N
    lane = lax.rem(c, mid)
    lane_piece = lax.div(lane, subs)
    is_low = c == mid - 1
    is_high = c == mid
    source = jnp.logical_or(is_low, c == mid - 2)
    near = c < mid - 2
    far = c > mid
    plain = jnp.logical_and(has_side, jnp.logical_not(jnp.logical_or(is_low, is_high)))
    gives = jnp.logical_and(jnp.logical_and(odd, c < n_ctx - 1), jnp.logical_not(is_low))
    gets = jnp.logical_and(odd, c < n_ctx - 1)
    takes = jnp.logical_and(even, c > 0)

    def cols(p):
        return pl.ds(pl.multiple_of(p * COLS, COLS), COLS)

    def piece(i):
        return lax.div(i, PIECES), pl.ds(pl.multiple_of(lax.rem(i, PIECES) * PIECE, PIECE), PIECE)

    def remote(src, dst, send, recv, place, head):
        return pltpu.make_async_remote_copy(
            src_ref=src, dst_ref=dst, send_sem=send, recv_sem=recv, device_id=(place, head), device_id_type=MESH
        )

    def mate_copy(i, src, dst, send, recv):
        a, rows = piece(i)
        return remote(src.at[a, rows], dst.at[a, rows], send.at[i], recv.at[i], mate, h)

    def side_copy(i, src, dst, send, recv):
        a, rows = piece(i)
        return remote(src.at[a, rows], dst.at[a, rows], send.at[i], recv.at[i], side, h)

    def part_of(i):
        a = lax.div(i, subs * PIECES)
        return a, pl.ds(pl.multiple_of(lax.rem(i, subs * PIECES) * (PIECE // subs), PIECE // subs), PIECE // subs)

    def send_parts():
        at = c - (mid - 2)

        def one(i, carry):
            a, rows = part_of(i)

            @pl.when(i < mid - 2)
            def _():
                remote(own.at[a, rows], hop.at[0, at], src_send.at[0], hop_recv.at[0], i, h).start()

            @pl.when(i >= mid - 2)
            def _():
                remote(own.at[a, rows], hop.at[1, at], src_send.at[0], hop_recv.at[1], mid + i, h).start()

            return carry

        lax.fori_loop(0, mid, one, 0)

    def give_grad(i):
        @pl.when(jnp.logical_and(takes, jnp.logical_not(is_high)))
        def _():
            side_copy(i, prev_g, next_in, ng_send, ng_recv).start()

        @pl.when(is_high)
        def _():
            for j in range(subs):
                to = i * subs + j
                a, rows = part_of(to)

                @pl.when(to > 0)
                def _():
                    remote(prev_g.at[a, rows], hop_g.at[0], ng_send.at[i], hop_recv.at[2], mid + to, h).start()

                @pl.when(to == 0)
                def _():
                    remote(prev_g.at[a, rows], hop_g.at[1], ng_send.at[i], hop_recv.at[3], 0, h).start()

    lane_a, lane_rows = part_of(lane)

    def arrived(k):
        ref = hop.at[k] if k < 2 else hop_g.at[k - 2]
        remote(ref, ref, hop_send.at[0], hop_recv.at[k], mid, h).wait_recv()

    def near_pair():
        return remote(hop.at[0], hop.at[1], hop_send.at[0], hop_recv.at[1], c + mid, h)

    def last_pair(k):
        return remote(hop.at[k], cand.at[:, lane_a, lane_rows], hop_send.at[k], cand_recv.at[lane_piece], mid, h)

    def far_grad():
        return remote(hop_g.at[0], hop_g.at[1], hop_send.at[2], hop_recv.at[3], c - mid, h)

    def last_grad(k):
        return remote(hop_g.at[k], next_in.at[lane_a, lane_rows], hop_send.at[2 + k], ng_recv.at[lane_piece], mid - 1, h)

    def h_tok(r):
        return peer_of(h, r) * toks

    def in_copy(k, r):
        src, dst = ((q_ref, qb), (g_ref, gb))[k]
        p = peer_of(h, r)
        return remote(src.at[:, cols(p)], dst.at[r], in_send.at[k, r], in_recv.at[k, r], c, p)

    def out_copy(k, r):
        src, dst = ((ob, att_ref), (db, dq_ref))[k]
        p = peer_of(h, r)
        return remote(src.at[r], dst.at[:, cols(h)], out_send.at[k, r], out_recv.at[k, r], c, p)

    barrier = pltpu.get_barrier_semaphore()
    for r in range(1, 8):
        pl.semaphore_signal(barrier, inc=1, device_id=(c, peer_of(h, r)), device_id_type=MESH)
    pl.semaphore_signal(barrier, inc=1, device_id=(mate, h), device_id_type=MESH)

    own_copies = [pltpu.make_async_copy(ref, own.at[a], own_sem.at[a]) for a, ref in enumerate((k_ref, v_ref))]
    own_tiles = [
        pltpu.make_async_copy(ref.at[:, cols(h)], buf.at[0], own_sem.at[2 + a])
        for a, (ref, buf) in enumerate(((q_ref, qb), (g_ref, gb)))
    ]
    for copy in own_copies + own_tiles:
        copy.start()

    def greet(place):
        pl.semaphore_signal(barrier, inc=1, device_id=(place, h), device_id_type=MESH)

    @pl.when(plain)
    def _():
        greet(side)

    def greet_all(places):
        def one(i, carry):
            greet(places(i))
            return carry

        lax.fori_loop(0, mid, one, 0)

    @pl.when(source)
    def _():
        greet_all(lambda i: jnp.where(i < mid - 2, i, i + mid))

    @pl.when(is_high)
    def _():
        greet_all(lambda i: jnp.where(i > 0, i + mid, 0))

    @pl.when(near)
    def _():
        greet(mid - 2)
        greet(mid - 1)
        greet(c + mid)

    @pl.when(far)
    def _():
        greet(mid)

    @pl.when(jnp.logical_and(far, c < n_ctx - 2))
    def _():
        greet(c - mid)

    @pl.when(c >= n_ctx - 2)
    def _():
        greet(mid - 2)
        greet(mid - 1)

    def count(condition, number):
        return jnp.where(condition, number, 0)

    last_two = c >= n_ctx - 2
    pl.semaphore_wait(
        barrier,
        8
        + count(plain, 1)
        + count(jnp.logical_or(source, is_high), mid)
        + count(jnp.logical_or(near, last_two), 3)
        + count(jnp.logical_and(far, jnp.logical_not(last_two)), 2),
    )

    for copy in own_copies:
        copy.wait()

    @pl.when(source)
    def _():
        send_parts()

    def send_own(i, carry):
        mate_copy(i, own, part, part_send, part_recv).start()
        return carry

    lax.fori_loop(0, N, send_own, 0)

    def send_in(*tiles):
        for r in tiles:
            for k in range(2):
                in_copy(k, r).start()

    send_in(1, 7, 6)

    @pl.when(near)
    def _():
        arrived(0)

        @pl.when(c > 0)
        def _():
            near_pair().start()

        @pl.when(c == 0)
        def _():
            last_pair(0).start()

    send_in(3, 2)

    flip_all = jnp.full((PIECE, HD), owner_ref[c], jnp.int32) != c
    flip_low = jnp.full((PIECE, HD), owner_ref[mid - 1], jnp.int32) != mid - 1
    n_low = jnp.sum((img_ref[...] < c).astype(jnp.int32), axis=1, keepdims=True)

    def set_half(a, rows, upper, value):
        for b, (both, both_t) in enumerate(((kk, kkt), (vv, vvt))):

            @pl.when(a == b)
            def _():
                cut = slice(HD, None) if upper else slice(0, HD)
                both[rows, cut] = value.astype(BF16)
                both_t[cut, rows] = jnp.transpose(value).astype(BF16)

    def take(i, carry):
        a, rows = piece(i)
        mate_copy(i, own, part, part_send, part_recv).wait_recv()
        mine = own[a, rows].astype(F32)
        other = part[a, rows].astype(F32)
        upper = jnp.where(flip_all, other, mine)

        @pl.when(odd)
        def _():
            fwd[a, rows] = upper.astype(BF16)

            @pl.when(gives)
            def _():
                side_copy(i, fwd, low, fwd_send, fwd_recv).start()

            set_half(a, rows, False, jnp.where(flip_all, mine, other))

        set_half(a, rows, True, upper)

        @pl.when(i == LATE)
        def _():
            send_in(5, 4)

        @pl.when(jnp.logical_and(far, i == RELAY))
        def _():
            arrived(1)
            last_pair(1).start()

        return carry

    lax.fori_loop(0, N, take, 0)

    @pl.when(even)
    def _():
        @pl.when(jnp.logical_not(takes))
        def _():
            low[...] = jnp.zeros_like(low)

        def arrive(i, carry):
            a, rows = piece(i)

            @pl.when(jnp.logical_and(takes, jnp.logical_not(is_high)))
            def _():
                side_copy(i, fwd, low, fwd_send, fwd_recv).wait_recv()

            @pl.when(is_high)
            def _():
                both = cand.at[:, a, rows]
                remote(both, both, hop_send.at[0], cand_recv.at[i], mid, h).wait_recv()
                low[a, rows] = jnp.where(flip_low, cand[0, a, rows].astype(F32), cand[1, a, rows].astype(F32)).astype(BF16)

            set_half(a, rows, False, low[a, rows].astype(F32))
            return carry

        lax.fori_loop(0, N, arrive, 0)

    def step(i, carry):
        t = jnp.where(i == 0, 0, jnp.where(i == 1, 3, i - 1))
        r = 2 * t

        @pl.when(t == 0)
        def _():
            for copy in own_tiles:
                copy.wait()

        @pl.when(t > 0)
        def _():
            for k in range(2):
                in_copy(k, r).wait_recv()

        for k in range(2):
            in_copy(k, r + 1).wait_recv()

        @pl.when(i == 3)
        def _():
            for r_out in (7, 6, 3, 2):
                for k in range(2):
                    out_copy(k, r_out).start()

        att, dq = pair_step(
            (qb[r], qb[r + 1]),
            (gb[r], gb[r + 1]),
            (h_tok(r), h_tok(r + 1)),
            n_low,
            kk,
            vv,
            kkt,
            vvt,
            ps.at[t],
            dss.at[t],
            qs.at[t],
            gs.at[t],
        )
        for j in range(2):
            ob[r + j] = att[j]
            db[r + j] = dq[j]

        @pl.when(t == 0)
        def _():
            for a, (buf, ref) in enumerate(((ob, att_ref), (db, dq_ref))):
                pltpu.make_async_copy(buf.at[0], ref.at[:, cols(h)], loc_sem.at[a]).start()
            for k in range(2):
                out_copy(k, 1).start()

        @pl.when(i == 3)
        def _():
            for r_out in (5, 4):
                for k in range(2):
                    out_copy(k, r_out).start()

        return carry

    lax.fori_loop(0, 4, step, 0)

    @pl.when(jnp.logical_and(odd, jnp.logical_not(gets)))
    def _():
        next_in[...] = jnp.zeros_like(next_in)

    for a, (left, right) in enumerate(((dss, qs), (ps, gs))):

        def sums(j, carry):
            i = a * PIECES + j
            rows = pl.ds(pl.multiple_of(j * PIECE, PIECE), PIECE)
            both = summed(left, right, rows)
            tot[...] = both * FACTOR if a == 0 else both

            @pl.when(even)
            def _():
                prev_g[a, rows] = tot[:, :HD].astype(BF16)
                give_grad(i)
                part_g[a, rows] = tot[:, HD:].astype(BF16)
                mate_copy(i, part_g, part_in, pg_send, pg_recv).start()
                fin[a, rows] = tot[:, HD:]

            @pl.when(odd)
            def _():
                @pl.when(gets)
                def _():
                    side_copy(i, prev_g, next_in, ng_send, ng_recv).wait_recv()

                lower = tot[:, :HD]
                upper = tot[:, HD:] + next_in[a, rows].astype(F32)
                part_g[a, rows] = jnp.where(flip_all, upper, lower).astype(BF16)
                mate_copy(i, part_g, part_in, pg_send, pg_recv).start()
                mate_copy(i, part_g, part_in, pg_send, pg_recv).wait_recv()
                other = part_in[a, rows].astype(F32)
                fin[a, rows] = jnp.where(flip_all, lower + other, upper)

            return carry

        lax.fori_loop(0, PIECES, sums, 0)

    @pl.when(far)
    def _():
        arrived(2)

        @pl.when(c < n_ctx - 1)
        def _():
            far_grad().start()

        @pl.when(c == n_ctx - 1)
        def _():
            last_grad(0).start()

    @pl.when(c < mid - 1)
    def _():
        arrived(3)
        last_grad(1).start()

    @pl.when(even)
    def _():
        def finish(i, carry):
            a, rows = piece(i)
            mate_copy(i, part_g, part_in, pg_send, pg_recv).wait_recv()
            other = part_in[a, rows].astype(F32)
            fin[a, rows] = jnp.where(flip_all, other, fin[a, rows] + other)
            return carry

        lax.fori_loop(0, N, finish, 0)

    outs = [pltpu.make_async_copy(fin.at[a], ref, loc_sem.at[2 + a]) for a, ref in enumerate((dk_ref, dv_ref))]
    for copy in outs:
        copy.start()

    def drain(i, carry):
        for k in range(2):
            in_copy(k, i).wait_send()
            out_copy(k, i).wait()
        return carry

    lax.fori_loop(1, 8, drain, 0)

    def drain_pieces(i, carry):
        mate_copy(i, own, part, part_send, part_recv).wait_send()
        mate_copy(i, part_g, part_in, pg_send, pg_recv).wait_send()

        @pl.when(gives)
        def _():
            side_copy(i, fwd, low, fwd_send, fwd_recv).wait_send()

        @pl.when(takes)
        def _():
            side_copy(i, prev_g, next_in, ng_send, ng_recv).wait_send()

        return carry

    lax.fori_loop(0, N, drain_pieces, 0)

    @pl.when(source)
    def _():
        remote(own, part, src_send.at[0], hop_recv.at[0], mid, h).wait_send()

    @pl.when(near)
    def _():
        near_pair().wait_send()

    @pl.when(c < mid - 1)
    def _():
        last_grad(1).wait_send()

    @pl.when(far)
    def _():
        last_pair(1).wait_send()
        far_grad().wait_send()

    for a, (buf, ref) in enumerate(((ob, att_ref), (db, dq_ref))):
        pltpu.make_async_copy(buf.at[0], ref.at[:, cols(h)], loc_sem.at[a]).wait()
    for copy in outs:
        copy.wait()


def per_device(n_ctx, query, d_out, keys_img, values_img, image_of, owner):
    toks = query.shape[0]
    anywhere = pl.BlockSpec(memory_space=pl.ANY)
    tile = pltpu.VMEM((8, toks, COLS), BF16)
    pair = pltpu.VMEM((2, ROWS, HD), BF16)
    part_rows = PIECE * N // (n_ctx // 2)
    dma = pltpu.SemaphoreType.DMA
    return pl.pallas_call(
        functools.partial(kernel, n_ctx),
        out_shape=(
            jax.ShapeDtypeStruct(query.shape, BF16),
            jax.ShapeDtypeStruct(query.shape, BF16),
            jax.ShapeDtypeStruct(keys_img.shape, F32),
            jax.ShapeDtypeStruct(values_img.shape, F32),
        ),
        in_specs=[anywhere] * 4
        + [pl.BlockSpec(memory_space=pltpu.VMEM), pl.BlockSpec(memory_space=pltpu.SMEM)],
        out_specs=(anywhere,) * 4,
        scratch_shapes=[tile] * 4
        + [pair] * 4
        + [pltpu.VMEM((ROWS, 2 * HD), BF16)] * 2
        + [pltpu.VMEM((2 * HD, ROWS), BF16)] * 2
        + [pltpu.VMEM((4, ROWS, 2 * GROUP * toks), BF16)] * 2
        + [pltpu.VMEM((4, 2 * GROUP * toks, 2 * HD), BF16)] * 2
        + [pair] * 4
        + [pltpu.VMEM((2, ROWS, HD), F32)]
        + [pltpu.VMEM((PIECE, 2 * HD), F32)]
        + [dma((4,))]
        + [dma((2, 8))] * 4
        + [dma((N,))] * 8
        + [dma((4,))]
        + [pltpu.VMEM((2, 2, part_rows, HD), BF16), pltpu.VMEM((2, part_rows, HD), BF16), pltpu.VMEM((2, 2, ROWS, HD), BF16)]
        + [dma((4,)), dma((4,)), dma((N,)), dma((1,))],
        compiler_params=pltpu.CompilerParams(collective_id=0, has_side_effects=True, vmem_limit_bytes=60 << 20),
        name="attend",
    )(query, d_out, keys_img, values_img, image_of.reshape(1, -1), owner)


def solution(mesh):
    placed = (
        P(("ctx", "head"), None),
        P(("ctx", "head"), None),
        P("ctx", "head"),
        P("ctx", "head"),
        P("ctx"),
        P(),
    )
    return jax.shard_map(
        functools.partial(per_device, mesh.shape["ctx"]),
        mesh=mesh,
        in_specs=placed,
        out_specs=(
            P(("ctx", "head"), None),
            P(("ctx", "head"), None),
            P("ctx", "head"),
            P("ctx", "head"),
        ),
        check_vma=False,
    )
```

time: 112 us -> 76 us (0.68)
  the two profiles are of different devices: /device:TPU:468 before, /device:TPU:460 now
where the time goes in v2:
time: 76 us; the launch traced here: 75.7 us
  Pallas kernels  69.8 us (92%)
  local copies, waits for them, and re-layouts  5.18 us (7%)
    pallas_call x1, Pallas kernels, per_device(): pl.pallas_call(functools.partial(kernel, n_ctx), out_shape=(jax.ShapeDtyp...  69.8 us
    unnamed x10, local copies, waits for them, and re-layouts  5.18 us

profile of v2, /device:TPU:460, one launch (start us, length us, event | category | flops | bytes accessed | tf_op | source)
XLA Modules:
  0.0 75.7 jit_solution(9671477554176855220)
XLA Ops:
  0.6 69.8 %attend.1 = (bf16[32,8192]{1,0:T(8,128)(2,1)}, bf16[32,8192]{1,0:T(8,128)(2,1)}, f32[1024,128]{1,0:T(8,128)}, f32[1024,128]{1,0:T(8,128)}) custom-call(bf16[32,8192]{1,0:T(8,128)(2,1)} %q_ref.1, bf16[32,8192]{1,0:T(8,128)(2,1)} %g_ref.1, bf16[1024,128]{1,0:T(8,128)(2,1)} %k_ref.1, bf16[1024,128]{1,0:T(8,128)(2,1)} %v_ref.1, s32[1,256]{1,0:T(1,128)} %bitcast.1, ...), custom_call_target="tpu_custom_call" | custom-call | tf_op jit(solution)/shard_map/attend/pallas_call | solution.py:613
  70.5 0.0 copy-start.2
  70.5 1.9 %copy.14 = bf16[32,8192]{1,0:T(8,128)(2,1)} copy(bf16[32,8192]{1,0:T(8,128)(2,1)} %get-tuple-element.8) | data formatting | bytes 1048576
  72.4 0.0 copy-done.2
  72.4 0.0 copy-start.1
  72.4 0.8 %copy.15 = bf16[32,8192]{1,0:T(8,128)(2,1)} copy(bf16[32,8192]{1,0:T(8,128)(2,1)S(1)} %copy-done.2) | data formatting | bytes 1048576
  73.2 0.4 copy-done.1
  73.7 0.0 copy-start
  73.7 0.8 %copy.16 = f32[1024,128]{1,0:T(8,128)} copy(f32[1024,128]{1,0:T(8,128)S(1)} %copy-done.1) | data formatting | bytes 1048576
  74.5 0.4 copy-done
  74.9 0.8 %copy.17 = f32[1024,128]{1,0:T(8,128)} copy(f32[1024,128]{1,0:T(8,128)S(1)} %copy-done) | data formatting | bytes 1048576
Async XLA Ops:
  70.5 1.9 %copy-start.2 = (bf16[32,8192]{1,0:T(8,128)(2,1)S(1)}, bf16[32,8192]{1,0:T(8,128)(2,1)}, u32[]{:S(2)}) copy-start(bf16[32,8192]{1,0:T(8,128)(2,1)} %get-tuple-element.9) | copy-start | bytes 1572868
  72.4 1.2 %copy-start.1 = (f32[1024,128]{1,0:T(8,128)S(1)}, f32[1024,128]{1,0:T(8,128)}, u32[]{:S(2)}) copy-start(f32[1024,128]{1,0:T(8,128)} %get-tuple-element.10) | copy-start | bytes 1572868
  73.7 1.2 %copy-start = (f32[1024,128]{1,0:T(8,128)S(1)}, f32[1024,128]{1,0:T(8,128)}, u32[]{:S(2)}) copy-start(f32[1024,128]{1,0:T(8,128)} %get-tuple-element.11) | copy-start | bytes 1572868

commit v3 on v2

--- a/solution.py
+++ b/solution.py
@@ -16,7 +16,9 @@
 N = 2 * PIECES
 FACTOR = HD**-0.5
 LOG2E = 1.4426950408889634
+CHUNKS = 2
 LATE, RELAY = 5, 5
+FAR_GRAD, NEAR_GRAD = 3, 7
 MESH = pl.DeviceIdType.MESH
 BF16 = jnp.bfloat16
 F32 = jnp.float32
@@ -164,7 +166,6 @@
     far = c > mid
     plain = jnp.logical_and(has_side, jnp.logical_not(jnp.logical_or(is_low, is_high)))
     gives = jnp.logical_and(jnp.logical_and(odd, c < n_ctx - 1), jnp.logical_not(is_low))
-    gets = jnp.logical_and(odd, c < n_ctx - 1)
     takes = jnp.logical_and(even, c > 0)
 
     def cols(p):
@@ -242,8 +243,33 @@
     def far_grad():
         return remote(hop_g.at[0], hop_g.at[1], hop_send.at[2], hop_recv.at[3], c - mid, h)
 
-    def last_grad(k):
-        return remote(hop_g.at[k], next_in.at[lane_a, lane_rows], hop_send.at[2 + k], ng_recv.at[lane_piece], mid - 1, h)
+    def last_grad(k, j):
+        ref = next_in.at[lane_a, lane_rows]
+        return remote(hop_g.at[k], ref, hop_send.at[3 + j], ng_recv.at[lane_piece], mid - 1 - j, h)
+
+    def pass_far_grad():
+        arrived(2)
+
+        @pl.when(c < n_ctx - 1)
+        def _():
+            far_grad().start()
+
+        @pl.when(c == n_ctx - 1)
+        def _():
+            for j in range(2):
+                last_grad(0, j).start()
+
+    def pass_near_grad():
+        arrived(3)
+        last_grad(1, 0).start()
+
+        @pl.when(near)
+        def _():
+            last_grad(1, 1).start()
+
+        @pl.when(c == mid - 2)
+        def _():
+            pltpu.make_async_copy(hop_g.at[1], next_in.at[lane_a, lane_rows], ng_recv.at[lane_piece]).start()
 
     def h_tok(r):
         return peer_of(h, r) * toks
@@ -486,10 +512,6 @@
 
     lax.fori_loop(0, 4, step, 0)
 
-    @pl.when(jnp.logical_and(odd, jnp.logical_not(gets)))
-    def _():
-        next_in[...] = jnp.zeros_like(next_in)
-
     for a, (left, right) in enumerate(((dss, qs), (ps, gs))):
 
         def sums(j, carry):
@@ -508,14 +530,24 @@
 
             @pl.when(odd)
             def _():
-                @pl.when(gets)
+                @pl.when(gives)
                 def _():
                     side_copy(i, prev_g, next_in, ng_send, ng_recv).wait_recv()
+                    tot[:, HD:] += next_in[a, rows].astype(F32)
 
                 lower = tot[:, :HD]
-                upper = tot[:, HD:] + next_in[a, rows].astype(F32)
+                upper = tot[:, HD:]
                 part_g[a, rows] = jnp.where(flip_all, upper, lower).astype(BF16)
                 mate_copy(i, part_g, part_in, pg_send, pg_recv).start()
+
+                @pl.when(jnp.logical_and(far, i == FAR_GRAD))
+                def _():
+                    pass_far_grad()
+
+                @pl.when(jnp.logical_and(near, i == NEAR_GRAD))
+                def _():
+                    pass_near_grad()
+
                 mate_copy(i, part_g, part_in, pg_send, pg_recv).wait_recv()
                 other = part_in[a, rows].astype(F32)
                 fin[a, rows] = jnp.where(flip_all, lower + other, upper)
@@ -524,25 +556,16 @@
 
         lax.fori_loop(0, PIECES, sums, 0)
 
-    @pl.when(far)
-    def _():
-        arrived(2)
-
-        @pl.when(c < n_ctx - 1)
-        def _():
-            far_grad().start()
-
-        @pl.when(c == n_ctx - 1)
-        def _():
-            last_grad(0).start()
-
-    @pl.when(c < mid - 1)
-    def _():
-        arrived(3)
-        last_grad(1).start()
-
     @pl.when(even)
     def _():
+        @pl.when(far)
+        def _():
+            pass_far_grad()
+
+        @pl.when(c < mid - 1)
+        def _():
+            pass_near_grad()
+
         def finish(i, carry):
             a, rows = piece(i)
             mate_copy(i, part_g, part_in, pg_send, pg_recv).wait_recv()
@@ -552,6 +575,19 @@
 
         lax.fori_loop(0, N, finish, 0)
 
+    @pl.when(source)
+    def _():
+        mine = flip_all == (jnp.full((PIECE, HD), c, jnp.int32) == mid - 2)
+
+        def finish(i, carry):
+            a, rows = piece(i)
+            remote(next_in.at[a, rows], next_in.at[a, rows], hop_send.at[0], ng_recv.at[i], mid, h).wait_recv()
+            other = next_in[a, rows].astype(F32)
+            fin[a, rows] += jnp.where(mine, other, jnp.zeros_like(other))
+            return carry
+
+        lax.fori_loop(0, N, finish, 0)
+
     outs = [pltpu.make_async_copy(fin.at[a], ref, loc_sem.at[2 + a]) for a, ref in enumerate((dk_ref, dv_ref))]
     for copy in outs:
         copy.start()
@@ -590,17 +626,49 @@
 
     @pl.when(c < mid - 1)
     def _():
-        last_grad(1).wait_send()
+        last_grad(1, 0).wait_send()
+
+    @pl.when(jnp.logical_or(near, c == n_ctx - 1))
+    def _():
+        last_grad(1, 1).wait_send()
 
     @pl.when(far)
     def _():
         last_pair(1).wait_send()
-        far_grad().wait_send()
+
+        @pl.when(c < n_ctx - 1)
+        def _():
+            far_grad().wait_send()
+
+        @pl.when(c == n_ctx - 1)
+        def _():
+            last_grad(0, 0).wait_send()
 
     for a, (buf, ref) in enumerate(((ob, att_ref), (db, dq_ref))):
         pltpu.make_async_copy(buf.at[0], ref.at[:, cols(h)], loc_sem.at[a]).wait()
     for copy in outs:
         copy.wait()
+
+
+def store(*refs):
+    sources, targets, held, (in_sem, out_sem) = refs[:4], refs[4:8], refs[8:12], refs[12:]
+
+    def copies(j, k):
+        size = sources[j].shape[0] // CHUNKS
+        rows = pl.ds(k * size, size)
+        return (
+            pltpu.make_async_copy(sources[j].at[rows], held[j].at[rows], in_sem.at[j, k]),
+            pltpu.make_async_copy(held[j].at[rows], targets[j].at[rows], out_sem.at[j, k]),
+        )
+
+    every = [copies(j, k) for k in range(CHUNKS) for j in range(4)]
+    for inward, _ in every:
+        inward.start()
+    for inward, outward in every:
+        inward.wait()
+        outward.start()
+    for _, outward in every:
+        outward.wait()
 
 
 def per_device(n_ctx, query, d_out, keys_img, values_img, image_of, owner):
@@ -610,7 +678,7 @@
     pair = pltpu.VMEM((2, ROWS, HD), BF16)
     part_rows = PIECE * N // (n_ctx // 2)
     dma = pltpu.SemaphoreType.DMA
-    return pl.pallas_call(
+    results = pl.pallas_call(
         functools.partial(kernel, n_ctx),
         out_shape=(
             jax.ShapeDtypeStruct(query.shape, BF16),
@@ -635,10 +703,18 @@
         + [dma((N,))] * 8
         + [dma((4,))]
         + [pltpu.VMEM((2, 2, part_rows, HD), BF16), pltpu.VMEM((2, part_rows, HD), BF16), pltpu.VMEM((2, 2, ROWS, HD), BF16)]
-        + [dma((4,)), dma((4,)), dma((N,)), dma((1,))],
+        + [dma((5,)), dma((4,)), dma((N,)), dma((1,))],
         compiler_params=pltpu.CompilerParams(collective_id=0, has_side_effects=True, vmem_limit_bytes=60 << 20),
         name="attend",
     )(query, d_out, keys_img, values_img, image_of.reshape(1, -1), owner)
+    return pl.pallas_call(
+        store,
+        out_shape=[jax.ShapeDtypeStruct(x.shape, x.dtype) for x in results],
+        in_specs=[anywhere] * 4,
+        out_specs=[anywhere] * 4,
+        scratch_shapes=[pltpu.VMEM(x.shape, x.dtype) for x in results] + [dma((4, CHUNKS))] * 2,
+        name="store",
+    )(*results)
 
 
 def solution(mesh):

time: 76 us -> 68.9 us (0.907)
  the two profiles are of different devices: /device:TPU:460 before, /device:TPU:56 now
where the time goes in v3:
time: 68.9 us; the launch traced here: 68.7 us
  Pallas kernels  68.1 us (99%)
    pallas_call x1, Pallas kernels, per_device(): pl.pallas_call(functools.partial(kernel, n_ctx), out_shape=(jax.ShapeDtyp...  65.7 us
    pallas_call x1, Pallas kernels, per_device(): pl.pallas_call(store, out_shape=[jax.ShapeDtypeStruct(x.shape, x.dtype) f...  2.4 us

profile of v3, /device:TPU:56, one launch (start us, length us, event | category | flops | bytes accessed | tf_op | source)
XLA Modules:
  0.0 68.7 jit_solution(6099662270095211951)
XLA Ops:
  0.6 65.7 %attend.1 = (bf16[32,8192]{1,0:T(8,128)(2,1)}, bf16[32,8192]{1,0:T(8,128)(2,1)}, f32[1024,128]{1,0:T(8,128)}, f32[1024,128]{1,0:T(8,128)}) custom-call(bf16[32,8192]{1,0:T(8,128)(2,1)} %q_ref.1, bf16[32,8192]{1,0:T(8,128)(2,1)} %g_ref.1, bf16[1024,128]{1,0:T(8,128)(2,1)} %k_ref.1, bf16[1024,128]{1,0:T(8,128)(2,1)} %v_ref.1, s32[1,256]{1,0:T(1,128)} %bitcast.1, ...), custom_call_target="tpu_custom_call" | custom-call | tf_op jit(solution)/shard_map/attend/pallas_call | solution.py:681
  66.3 2.4 %store.1 = (bf16[32,8192]{1,0:T(8,128)(2,1)}, bf16[32,8192]{1,0:T(8,128)(2,1)}, f32[1024,128]{1,0:T(8,128)}, f32[1024,128]{1,0:T(8,128)}) custom-call(bf16[32,8192]{1,0:T(8,128)(2,1)} %get-tuple-element.8.refs_0_, bf16[32,8192]{1,0:T(8,128)(2,1)} %get-tuple-element.9.refs_1_, f32[1024,128]{1,0:T(8,128)} %get-tuple-element.10.refs_2_, ...), custom_call_target="tpu_custom_call" | custom-call | tf_op jit(solution)/shard_map/store/pallas_call | solution.py:710

commit v4 on v3

--- a/solution.py
+++ b/solution.py
@@ -17,7 +17,7 @@
 FACTOR = HD**-0.5
 LOG2E = 1.4426950408889634
 CHUNKS = 2
-LATE, RELAY = 5, 5
+LATE = 5
 FAR_GRAD, NEAR_GRAD = 3, 7
 MESH = pl.DeviceIdType.MESH
 BF16 = jnp.bfloat16
@@ -140,8 +140,8 @@
     ng_recv,
     loc_sem,
     hop,
+    chosen,
     hop_g,
-    cand,
     hop_send,
     hop_recv,
     cand_recv,
@@ -199,11 +199,11 @@
 
             @pl.when(i < mid - 2)
             def _():
-                remote(own.at[a, rows], hop.at[0, at], src_send.at[0], hop_recv.at[0], i, h).start()
+                remote(own.at[a, rows], hop.at[at], src_send.at[0], hop_recv.at[0], i, h).start()
 
             @pl.when(i >= mid - 2)
             def _():
-                remote(own.at[a, rows], hop.at[1, at], src_send.at[0], hop_recv.at[1], mid + i, h).start()
+                remote(own.at[a, rows], hop.at[at], src_send.at[0], hop_recv.at[0], mid + i, h).start()
 
             return carry
 
@@ -231,14 +231,42 @@
     lane_a, lane_rows = part_of(lane)
 
     def arrived(k):
-        ref = hop.at[k] if k < 2 else hop_g.at[k - 2]
+        ref = hop if k == 0 else chosen if k == 1 else hop_g.at[k - 2]
         remote(ref, ref, hop_send.at[0], hop_recv.at[k], mid, h).wait_recv()
 
+    def choose():
+        flipped = jnp.full(chosen.shape, owner_ref[mid - 1], jnp.int32) != mid - 1
+        chosen[...] = jnp.where(flipped, hop[0].astype(F32), hop[1].astype(F32)).astype(BF16)
+
     def near_pair():
-        return remote(hop.at[0], hop.at[1], hop_send.at[0], hop_recv.at[1], c + mid, h)
-
-    def last_pair(k):
-        return remote(hop.at[k], cand.at[:, lane_a, lane_rows], hop_send.at[k], cand_recv.at[lane_piece], mid, h)
+        return remote(chosen, chosen, hop_send.at[0], hop_recv.at[1], c + mid, h)
+
+    def last_pair():
+        return remote(chosen, low.at[lane_a, lane_rows], hop_send.at[1], cand_recv.at[lane_piece], mid, h)
+
+    def pass_near():
+        arrived(0)
+        choose()
+
+        @pl.when(c > 0)
+        def _():
+            near_pair().start()
+
+        @pl.when(c == 0)
+        def _():
+            last_pair().start()
+
+    def pass_far():
+        @pl.when(c < n_ctx - 2)
+        def _():
+            arrived(1)
+
+        @pl.when(c >= n_ctx - 2)
+        def _():
+            arrived(0)
+            choose()
+
+        last_pair().start()
 
     def far_grad():
         return remote(hop_g.at[0], hop_g.at[1], hop_send.at[2], hop_recv.at[3], c - mid, h)
@@ -311,44 +339,24 @@
 
         lax.fori_loop(0, mid, one, 0)
 
-    @pl.when(source)
-    def _():
-        greet_all(lambda i: jnp.where(i < mid - 2, i, i + mid))
-
     @pl.when(is_high)
     def _():
         greet_all(lambda i: jnp.where(i > 0, i + mid, 0))
 
-    @pl.when(near)
+    @pl.when(jnp.logical_or(near, c >= n_ctx - 2))
     def _():
         greet(mid - 2)
         greet(mid - 1)
-        greet(c + mid)
-
-    @pl.when(far)
-    def _():
-        greet(mid)
 
     @pl.when(jnp.logical_and(far, c < n_ctx - 2))
     def _():
         greet(c - mid)
-
-    @pl.when(c >= n_ctx - 2)
-    def _():
-        greet(mid - 2)
-        greet(mid - 1)
 
     def count(condition, number):
         return jnp.where(condition, number, 0)
 
-    last_two = c >= n_ctx - 2
     pl.semaphore_wait(
-        barrier,
-        8
-        + count(plain, 1)
-        + count(jnp.logical_or(source, is_high), mid)
-        + count(jnp.logical_or(near, last_two), 3)
-        + count(jnp.logical_and(far, jnp.logical_not(last_two)), 2),
+        barrier, 8 + count(plain, 1) + count(source, mid) + count(jnp.logical_or(near, far), 1)
     )
 
     for copy in own_copies:
@@ -369,24 +377,9 @@
             for k in range(2):
                 in_copy(k, r).start()
 
-    send_in(1, 7, 6)
-
-    @pl.when(near)
-    def _():
-        arrived(0)
-
-        @pl.when(c > 0)
-        def _():
-            near_pair().start()
-
-        @pl.when(c == 0)
-        def _():
-            last_pair(0).start()
-
-    send_in(3, 2)
+    send_in(1, 7, 6, 3, 2)
 
     flip_all = jnp.full((PIECE, HD), owner_ref[c], jnp.int32) != c
-    flip_low = jnp.full((PIECE, HD), owner_ref[mid - 1], jnp.int32) != mid - 1
     n_low = jnp.sum((img_ref[...] < c).astype(jnp.int32), axis=1, keepdims=True)
 
     def set_half(a, rows, upper, value):
@@ -397,6 +390,9 @@
                 cut = slice(HD, None) if upper else slice(0, HD)
                 both[rows, cut] = value.astype(BF16)
                 both_t[cut, rows] = jnp.transpose(value).astype(BF16)
+
+    near_turn = jnp.maximum(N - 2 - lane_piece, 0)
+    far_turn = jnp.minimum(N - 1 - lax.div(lane_piece - 3 + 8, 2) + 4, N - 1)
 
     def take(i, carry):
         a, rows = piece(i)
@@ -421,10 +417,13 @@
         def _():
             send_in(5, 4)
 
-        @pl.when(jnp.logical_and(far, i == RELAY))
-        def _():
-            arrived(1)
-            last_pair(1).start()
+        @pl.when(jnp.logical_and(near, i == near_turn))
+        def _():
+            pass_near()
+
+        @pl.when(jnp.logical_and(far, i == far_turn))
+        def _():
+            pass_far()
 
         return carry
 
@@ -445,9 +444,7 @@
 
             @pl.when(is_high)
             def _():
-                both = cand.at[:, a, rows]
-                remote(both, both, hop_send.at[0], cand_recv.at[i], mid, h).wait_recv()
-                low[a, rows] = jnp.where(flip_low, cand[0, a, rows].astype(F32), cand[1, a, rows].astype(F32)).astype(BF16)
+                remote(low.at[a, rows], low.at[a, rows], hop_send.at[0], cand_recv.at[i], mid, h).wait_recv()
 
             set_half(a, rows, False, low[a, rows].astype(F32))
             return carry
@@ -471,7 +468,7 @@
         for k in range(2):
             in_copy(k, r + 1).wait_recv()
 
-        @pl.when(i == 3)
+        @pl.when(jnp.logical_and(i == 3, jnp.logical_not(is_high)))
         def _():
             for r_out in (7, 6, 3, 2):
                 for k in range(2):
@@ -502,11 +499,11 @@
             for k in range(2):
                 out_copy(k, 1).start()
 
-        @pl.when(i == 3)
-        def _():
-            for r_out in (5, 4):
+        @pl.when(jnp.logical_or(i == 3, jnp.logical_and(is_high, i > 0)))
+        def _():
+            for j in (1, 0):
                 for k in range(2):
-                    out_copy(k, r_out).start()
+                    out_copy(k, r + j).start()
 
         return carry
 
@@ -620,10 +617,14 @@
     def _():
         remote(own, part, src_send.at[0], hop_recv.at[0], mid, h).wait_send()
 
-    @pl.when(near)
+    @pl.when(jnp.logical_and(near, c > 0))
     def _():
         near_pair().wait_send()
 
+    @pl.when(jnp.logical_or(c == 0, far))
+    def _():
+        last_pair().wait_send()
+
     @pl.when(c < mid - 1)
     def _():
         last_grad(1, 0).wait_send()
@@ -634,8 +635,6 @@
 
     @pl.when(far)
     def _():
-        last_pair(1).wait_send()
-
         @pl.when(c < n_ctx - 1)
         def _():
             far_grad().wait_send()
@@ -702,7 +701,7 @@
         + [dma((2, 8))] * 4
         + [dma((N,))] * 8
         + [dma((4,))]
-        + [pltpu.VMEM((2, 2, part_rows, HD), BF16), pltpu.VMEM((2, part_rows, HD), BF16), pltpu.VMEM((2, 2, ROWS, HD), BF16)]
+        + [pltpu.VMEM((2, part_rows, HD), BF16), pltpu.VMEM((part_rows, HD), BF16), pltpu.VMEM((2, part_rows, HD), BF16)]
         + [dma((5,)), dma((4,)), dma((N,)), dma((1,))],
         compiler_params=pltpu.CompilerParams(collective_id=0, has_side_effects=True, vmem_limit_bytes=60 << 20),
         name="attend",

time: 68.9 us -> 67.7 us (0.983)
  Pallas kernels: 68.1 us -> 66.8 us
    pallas_call x1, Pallas kernels: 65.7 us -> 64.4 us  [per_device(): pl.pallas_call(functools.partial(kernel, n_ctx), out_shape=(jax.ShapeDtyp...]
where the time goes in v4:
time: 67.7 us; the launch traced here: 67.5 us
  Pallas kernels  66.8 us (99%)
    pallas_call x1, Pallas kernels, per_device(): pl.pallas_call(functools.partial(kernel, n_ctx), out_shape=(jax.ShapeDtyp...  64.4 us
    pallas_call x1, Pallas kernels, per_device(): pl.pallas_call(store, out_shape=[jax.ShapeDtypeStruct(x.shape, x.dtype) f...  2.4 us

profile of v4, /device:TPU:56, one launch (start us, length us, event | category | flops | bytes accessed | tf_op | source)
XLA Modules:
  0.0 67.5 jit_solution(13947587490062607798)
XLA Ops:
  0.6 64.4 %attend.1 = (bf16[32,8192]{1,0:T(8,128)(2,1)}, bf16[32,8192]{1,0:T(8,128)(2,1)}, f32[1024,128]{1,0:T(8,128)}, f32[1024,128]{1,0:T(8,128)}) custom-call(bf16[32,8192]{1,0:T(8,128)(2,1)} %q_ref.1, bf16[32,8192]{1,0:T(8,128)(2,1)} %g_ref.1, bf16[1024,128]{1,0:T(8,128)(2,1)} %k_ref.1, bf16[1024,128]{1,0:T(8,128)(2,1)} %v_ref.1, s32[1,256]{1,0:T(1,128)} %bitcast.1, ...), custom_call_target="tpu_custom_call" | custom-call | tf_op jit(solution)/shard_map/attend/pallas_call | solution.py:680
  65.1 2.4 %store.1 = (bf16[32,8192]{1,0:T(8,128)(2,1)}, bf16[32,8192]{1,0:T(8,128)(2,1)}, f32[1024,128]{1,0:T(8,128)}, f32[1024,128]{1,0:T(8,128)}) custom-call(bf16[32,8192]{1,0:T(8,128)(2,1)} %get-tuple-element.8.refs_0_, bf16[32,8192]{1,0:T(8,128)(2,1)} %get-tuple-element.9.refs_1_, f32[1024,128]{1,0:T(8,128)} %get-tuple-element.10.refs_2_, ...), custom_call_target="tpu_custom_call" | custom-call | tf_op jit(solution)/shard_map/store/pallas_call | solution.py:709

commit v5 on v4

--- a/solution.py
+++ b/solution.py
@@ -370,14 +370,25 @@
         mate_copy(i, own, part, part_send, part_recv).start()
         return carry
 
-    lax.fori_loop(0, N, send_own, 0)
+    @pl.when(jnp.logical_not(source))
+    def _():
+        lax.fori_loop(0, N, send_own, 0)
 
     def send_in(*tiles):
         for r in tiles:
             for k in range(2):
                 in_copy(k, r).start()
 
-    send_in(1, 7, 6, 3, 2)
+    send_in(1, 7, 6)
+
+    @pl.when(jnp.logical_not(near))
+    def _():
+        send_in(3, 2)
+
+    @pl.when(source)
+    def _():
+        remote(own, part, src_send.at[0], hop_recv.at[0], mid, h).wait_send()
+        lax.fori_loop(0, N, send_own, 0)
 
     flip_all = jnp.full((PIECE, HD), owner_ref[c], jnp.int32) != c
     n_low = jnp.sum((img_ref[...] < c).astype(jnp.int32), axis=1, keepdims=True)
@@ -392,6 +403,7 @@
                 both_t[cut, rows] = jnp.transpose(value).astype(BF16)
 
     near_turn = jnp.maximum(N - 2 - lane_piece, 0)
+    late_turn = jnp.where(near, jnp.maximum(near_turn, LATE), LATE)
     far_turn = jnp.minimum(N - 1 - lax.div(lane_piece - 3 + 8, 2) + 4, N - 1)
 
     def take(i, carry):
@@ -413,13 +425,14 @@
 
         set_half(a, rows, True, upper)
 
-        @pl.when(i == LATE)
+        @pl.when(jnp.logical_and(near, i == near_turn))
+        def _():
+            pass_near()
+            send_in(3, 2)
+
+        @pl.when(i == late_turn)
         def _():
             send_in(5, 4)
-
-        @pl.when(jnp.logical_and(near, i == near_turn))
-        def _():
-            pass_near()
 
         @pl.when(jnp.logical_and(far, i == far_turn))
         def _():
@@ -612,10 +625,6 @@
         return carry
 
     lax.fori_loop(0, N, drain_pieces, 0)
-
-    @pl.when(source)
-    def _():
-        remote(own, part, src_send.at[0], hop_recv.at[0], mid, h).wait_send()
 
     @pl.when(jnp.logical_and(near, c > 0))
     def _():

time: 67.7 us -> 64.6 us (0.954)
  Pallas kernels: 66.8 us -> 63.8 us
    pallas_call x1, Pallas kernels: 64.4 us -> 61.4 us  [per_device(): pl.pallas_call(functools.partial(kernel, n_ctx), out_shape=(jax.ShapeDtyp...]
where the time goes in v5:
time: 64.6 us; the launch traced here: 64.5 us
  Pallas kernels  63.8 us (99%)
    pallas_call x1, Pallas kernels, per_device(): pl.pallas_call(functools.partial(kernel, n_ctx), out_shape=(jax.ShapeDtyp...  61.4 us
    pallas_call x1, Pallas kernels, per_device(): pl.pallas_call(store, out_shape=[jax.ShapeDtypeStruct(x.shape, x.dtype) f...  2.4 us

profile of v5, /device:TPU:56, one launch (start us, length us, event | category | flops | bytes accessed | tf_op | source)
XLA Modules:
  0.0 64.5 jit_solution(12270745710380731729)
XLA Ops:
  0.6 61.4 %attend.1 = (bf16[32,8192]{1,0:T(8,128)(2,1)}, bf16[32,8192]{1,0:T(8,128)(2,1)}, f32[1024,128]{1,0:T(8,128)}, f32[1024,128]{1,0:T(8,128)}) custom-call(bf16[32,8192]{1,0:T(8,128)(2,1)} %q_ref.1, bf16[32,8192]{1,0:T(8,128)(2,1)} %g_ref.1, bf16[1024,128]{1,0:T(8,128)(2,1)} %k_ref.1, bf16[1024,128]{1,0:T(8,128)(2,1)} %v_ref.1, s32[1,256]{1,0:T(1,128)} %bitcast.1, ...), custom_call_target="tpu_custom_call" | custom-call | tf_op jit(solution)/shard_map/attend/pallas_call | solution.py:689
  62.1 2.4 %store.1 = (bf16[32,8192]{1,0:T(8,128)(2,1)}, bf16[32,8192]{1,0:T(8,128)(2,1)}, f32[1024,128]{1,0:T(8,128)}, f32[1024,128]{1,0:T(8,128)}) custom-call(bf16[32,8192]{1,0:T(8,128)(2,1)} %get-tuple-element.8.refs_0_, bf16[32,8192]{1,0:T(8,128)(2,1)} %get-tuple-element.9.refs_1_, f32[1024,128]{1,0:T(8,128)} %get-tuple-element.10.refs_2_, ...), custom_call_target="tpu_custom_call" | custom-call | tf_op jit(solution)/shard_map/store/pallas_call | solution.py:718

commit v6 on v5

--- a/solution.py
+++ b/solution.py
@@ -402,7 +402,7 @@
                 both[rows, cut] = value.astype(BF16)
                 both_t[cut, rows] = jnp.transpose(value).astype(BF16)
 
-    near_turn = jnp.maximum(N - 2 - lane_piece, 0)
+    near_turn = jnp.maximum(N - 3 - lane_piece, 0)
     late_turn = jnp.where(near, jnp.maximum(near_turn, LATE), LATE)
     far_turn = jnp.minimum(N - 1 - lax.div(lane_piece - 3 + 8, 2) + 4, N - 1)
 

time: 64.6 us -> 64.6 us (level)
  no operation moved by 1% of the time
where the time goes in v6:
time: 64.6 us; the launch traced here: 64.5 us
  Pallas kernels  63.8 us (99%)
    pallas_call x1, Pallas kernels, per_device(): pl.pallas_call(functools.partial(kernel, n_ctx), out_shape=(jax.ShapeDtyp...  61.4 us
    pallas_call x1, Pallas kernels, per_device(): pl.pallas_call(store, out_shape=[jax.ShapeDtypeStruct(x.shape, x.dtype) f...  2.4 us

profile of v6, /device:TPU:56, one launch (start us, length us, event | category | flops | bytes accessed | tf_op | source)
XLA Modules:
  0.0 64.5 jit_solution(5294127408289369533)
XLA Ops:
  0.6 61.4 %attend.1 = (bf16[32,8192]{1,0:T(8,128)(2,1)}, bf16[32,8192]{1,0:T(8,128)(2,1)}, f32[1024,128]{1,0:T(8,128)}, f32[1024,128]{1,0:T(8,128)}) custom-call(bf16[32,8192]{1,0:T(8,128)(2,1)} %q_ref.1, bf16[32,8192]{1,0:T(8,128)(2,1)} %g_ref.1, bf16[1024,128]{1,0:T(8,128)(2,1)} %k_ref.1, bf16[1024,128]{1,0:T(8,128)(2,1)} %v_ref.1, s32[1,256]{1,0:T(1,128)} %bitcast.1, ...), custom_call_target="tpu_custom_call" | custom-call | tf_op jit(solution)/shard_map/attend/pallas_call | solution.py:689
  62.1 2.4 %store.1 = (bf16[32,8192]{1,0:T(8,128)(2,1)}, bf16[32,8192]{1,0:T(8,128)(2,1)}, f32[1024,128]{1,0:T(8,128)}, f32[1024,128]{1,0:T(8,128)}) custom-call(bf16[32,8192]{1,0:T(8,128)(2,1)} %get-tuple-element.8.refs_0_, bf16[32,8192]{1,0:T(8,128)(2,1)} %get-tuple-element.9.refs_1_, f32[1024,128]{1,0:T(8,128)} %get-tuple-element.10.refs_2_, ...), custom_call_target="tpu_custom_call" | custom-call | tf_op jit(solution)/shard_map/store/pallas_call | solution.py:718
